TPU v7x, 256 devices: a whole 4x4x8 slice. The times are simulated.
256 devices in a mesh: rep: 32 (over x, z_hi, core), dom: 8 (over z_lo, y).
Axes of the slice: x: 4, y: 4, z: 8 (z_hi: 4, z_lo: 2; z = z_hi * 2 + z_lo), core: 2. Of those that a mesh axis runs over, the one named last changes fastest.
Arguments:
- tokens: bfloat16 [131072, 1792], P(('rep', 'dom')), may hold values from -6 to 6
- routes: int32 [131072, 8], P(('rep', 'dom')), may hold values from 0 to 63, as said below
- gate_codes: int32 [131072, 8], P(('rep', 'dom')), may hold values from 1 to 64
- cotangent: bfloat16 [131072, 1792], P(('rep', 'dom')), may hold values from -48 to 48
- w_gate: bfloat16 [1792, 1280], P('dom'), may hold values from -0.125 to 0.125
- w_up: bfloat16 [1792, 1280], P('dom'), may hold values from -0.125 to 0.125
- w_down: bfloat16 [1792, 1280], P('dom'), may hold values from -0.15625 to 0.15625
Outputs:
- d_tokens: bfloat16 [131072, 1792], P(('rep', 'dom'))
- grad_gate: float32 [1792, 1280], P('dom')
- grad_up: float32 [1792, 1280], P('dom')
- grad_down: float32 [1792, 1280], P('dom')
Inputs may be any that keep to these rules, and one draw needn't show every extreme that they name: `routes`: each row names 8 different experts. In each aligned block of 512 rows (the rows of one device) between 48 and 96 rows name expert 0, and in every draw some block has exactly 96 such rows.
All inputs are finite; a program needn't handle non-finite values.
Results may differ from a plain program's by a relative error of at most 0.015.
Values may be sent and summed in bfloat16 or wider, within the bound.
A program may use at most 128 MiB of HBM per device.

v0:
```python
import jax
import jax.numpy as jnp
from jax import lax
from jax.sharding import PartitionSpec as P

CAP = 96


def matmul(left, right):
    return jnp.dot(left, right, preferred_element_type=jnp.float32)


def times_transpose_exact(left, right):
    return lax.dot_general(
        left,
        right.astype(jnp.float32),
        (((1,), (1,)), ((), ())),
        precision=lax.Precision.HIGHEST,
        preferred_element_type=jnp.float32,
    )


def transpose_times(left, right):
    return lax.dot_general(
        left, right, (((0,), (0,)), ((), ())), preferred_element_type=jnp.float32
    )


def transpose_times_exact(left, right):
    return lax.dot_general(
        left.astype(jnp.float32),
        right,
        (((0,), (0,)), ((), ())),
        precision=lax.Precision.HIGHEST,
        preferred_element_type=jnp.float32,
    )


def pick_rows(tokens, routes, gate_codes, cotangent):
    token_count = tokens.shape[0]
    member = routes == 0
    routed = jnp.any(member, axis=1)
    gate_weight = jnp.sum(jnp.where(member, gate_codes, 0), axis=1).astype(jnp.float32) / 256.0
    chosen = jnp.nonzero(routed, size=CAP, fill_value=token_count)[0].astype(jnp.int32)
    usable = chosen < token_count
    clipped = jnp.minimum(chosen, token_count - 1).astype(jnp.int32)
    picked = jnp.where(usable[:, None], tokens[clipped], jnp.zeros((), jnp.bfloat16))
    weight_rows = jnp.where(usable, gate_weight[clipped], jnp.zeros((), jnp.float32))
    scaled = (weight_rows[:, None] * cotangent[clipped].astype(jnp.float32)).astype(jnp.bfloat16)
    return (chosen, picked, scaled)


def swiglu_parts(pre_gate, pre_up):
    sigmoid_gate = jax.nn.sigmoid(pre_gate)
    activated = pre_gate * sigmoid_gate
    hidden = (activated * pre_up).astype(jnp.bfloat16)
    return (sigmoid_gate, activated, hidden)


def swiglu_back(d_hidden, pre_gate, pre_up, sigmoid_gate, activated):
    d_gate = d_hidden * pre_up * sigmoid_gate * (1.0 + pre_gate * (1.0 - sigmoid_gate))
    d_up = d_hidden * activated
    return (d_gate, d_up)


def local_expert(picked, scaled, full_gate, full_up, full_down):
    pre_gate = matmul(picked, full_gate)
    pre_up = matmul(picked, full_up)
    sigmoid_gate, activated, hidden = swiglu_parts(pre_gate, pre_up)
    d_hidden = matmul(scaled, full_down)
    d_gate, d_up = swiglu_back(d_hidden, pre_gate, pre_up, sigmoid_gate, activated)
    d_picked = (
        times_transpose_exact(d_gate, full_gate) + times_transpose_exact(d_up, full_up)
    ).astype(jnp.bfloat16)
    return (hidden, d_gate, d_up, d_picked)


def body(tokens, routes, gate_codes, cotangent, w_gate, w_up, w_down):
    chosen, picked, scaled = pick_rows(tokens, routes, gate_codes, cotangent)
    hidden_width = w_gate.shape[1]
    full_gate, full_up, full_down = (
        lax.all_gather(w_gate, "dom", axis=0, tiled=True),
        lax.all_gather(w_up, "dom", axis=0, tiled=True),
        lax.all_gather(w_down, "dom", axis=0, tiled=True),
    )
    hidden, d_gate, d_up, d_picked = local_expert(picked, scaled, full_gate, full_up, full_down)
    length = lax.axis_size("dom") * w_gate.shape[0]
    picked_cols = lax.slice_in_dim(picked, 0, length, axis=1)
    scaled_cols = lax.slice_in_dim(scaled, 0, length, axis=1)
    group_shard = lax.psum_scatter(
        jnp.concatenate(
            [
                transpose_times_exact(picked_cols, d_gate),
                transpose_times_exact(picked_cols, d_up),
                transpose_times(scaled_cols, hidden),
            ],
            axis=1,
        ).astype(jnp.bfloat16),
        "dom",
        scatter_dimension=0,
        tiled=True,
    ).astype(jnp.float32)
    totals = lax.psum(group_shard, "rep")
    grad_gate = totals[:, :hidden_width]
    grad_up = totals[:, hidden_width : 2 * hidden_width]
    grad_down = totals[:, 2 * hidden_width :]
    d_tokens = jnp.zeros(tokens.shape, jnp.bfloat16).at[chosen].set(d_picked, mode="drop")
    return (d_tokens, grad_gate, grad_up, grad_down)


def solution(mesh):
    placed = (
        P(("rep", "dom"), None),
        P(("rep", "dom"), None),
        P(("rep", "dom"), None),
        P(("rep", "dom"), None),
        P("dom", None),
        P("dom", None),
        P("dom", None),
    )
    return jax.shard_map(
        body,
        mesh=mesh,
        in_specs=placed,
        out_specs=(P(("rep", "dom"), None), P("dom", None), P("dom", None), P("dom", None)),
        check_vma=False,
    )
```

profile of v0, /device:TPU:1, one launch (start us, length us, event | category | flops | bytes accessed | tf_op | source)
XLA Modules:
  0.0 569.5 jit_solution(12807460900272346874)
XLA Ops:
  10.9 4.1 scatter_custom_fusion
  16.6 1.3 gather_fusion
  18.7 2.9 gather_fusion.1
  22.3 50.3 %all-gather.8.cloned.1.call-done = bf16[1792,1280]{1,0:T(8,128)(2,1)} async-done(((bf16[224,1280]{1,0:T(8,128)(2,1)}), bf16[1792,1280]{1,0:T(8,128)(2,1)}) %all-gather.8.cloned.1.call-update) | async-done | bytes 4587536 | tf_op jit(solution)/shard_map/all_gather | solution.py:82
  72.6 3.2 fusion.15
  75.8 56.2 %all-gather.6.cloned.1.call-done = bf16[1792,1280]{1,0:T(8,128)(2,1)} async-done(((bf16[224,1280]{1,0:T(8,128)(2,1)}), bf16[1792,1280]{1,0:T(8,128)(2,1)}) %all-gather.6.cloned.1.call-update) | async-done | bytes 4587536 | tf_op jit(solution)/shard_map/all_gather | solution.py:83
  132.0 3.2 fusion.16
  135.3 3.6 convolution_convert_fusion
  138.8 52.7 %all-gather.4.cloned.1.call-done = bf16[1792,1280]{1,0:T(8,128)(2,1)} async-done(((bf16[224,1280]{1,0:T(8,128)(2,1)}), bf16[1792,1280]{1,0:T(8,128)(2,1)}) %all-gather.4.cloned.1.call-update) | async-done | bytes 4587536 | tf_op jit(solution)/shard_map/all_gather | solution.py:84
  191.5 3.4 fusion.6
  194.9 4.1 convolution_convert_fusion.2
  199.0 4.1 convolution_convert_fusion.1
  203.1 5.9 %pad_maximum_fusion = bf16[1792,3840]{0,1:T(8,128)(2,1)} fusion(bf16[1792,1280]{0,1:T(8,128)(2,1)S(1)} %bitcast.13, bf16[1792,1280]{0,1:T(8,128)(2,1)S(1)} %convolution_convert_fusion.1, bf16[1792,1280]{0,1:T(8,128)(2,1)S(1)} %convolution_convert_fusion.2), kind=kLoop, calls=%fused_computation.5 | loop fusion | flops 41287680 | bytes 27525120 | tf_op jit(solution)/shard_map/concatenate | solution.py:91
  209.0 18.3 %copy.23 = bf16[1792,3840]{1,0:T(8,128)(2,1)} copy(bf16[1792,3840]{0,1:T(8,128)(2,1)} %pad_maximum_fusion) | data formatting | bytes 27525120
  227.4 6.1 %fusion.20 = f32[96,1792]{1,0:T(8,128)S(1)} fusion(bf16[1792,1280]{1,0:T(8,128)(2,1)} %all-gather.8.cloned.1.call-done, f32[96,1280]{1,0:T(8,128)S(1)} %fusion.15, f32[96,1280]{1,0:T(8,128)S(1)} %fusion.6, f32[96,1280]{1,0:T(8,128)S(1)} %fusion.16), kind=kOutput, calls=%fused_computation.52 | convolution fusion | flops 2643517440 | bytes 6750208 | tf_op jit(solution)/shard_map/dot_general | solution.py:14
  233.4 6.5 %fusion = bf16[96,1792]{1,0:T(8,128)(2,1)S(1)} fusion(f32[96,1792]{1,0:T(8,128)S(1)} %fusion.20, bf16[1792,1280]{1,0:T(8,128)(2,1)} %all-gather.6.cloned.1.call-done, f32[96,1280]{1,0:T(8,128)S(1)} %fusion.6, f32[96,1280]{1,0:T(8,128)S(1)} %fusion.15), kind=kOutput, calls=%fused_computation.10 | convolution fusion | flops 2643369984 | bytes 6602752 | tf_op jit(solution)/shard_map/dot_general | solution.py:14
  240.0 2.7 scatter_custom_fusion.1
  242.6 129.8 %reduce-scatter.4.cloned.1.call-done = bf16[224,3840]{1,0:T(8,128)(2,1)} async-done(((bf16[1792,3840]{1,0:T(8,128)(2,1)}), bf16[224,3840]{1,0:T(8,128)(2,1)}) %reduce-scatter.4.cloned.1.call-update) | async-done | bytes 1720336
  372.4 3.9 copy.24
  376.2 175.9 %all-reduce.1 = f32[224,3840]{0,1:T(8,128)} all-reduce(bf16[224,3840]{0,1:T(8,128)(2,1)} %copy.24), channel_id=1, replica_groups=mesh['rep'=32,'dom'=8] {'rep'}, use_global_device_ids=true, to_apply=%region_9.10 | all-reduce | flops 860160 | bytes 5160960 | tf_op jit(solution)/shard_map/psum | solution.py:103
  552.2 4.0 fusion.23
  556.2 2.7 copy.22
  558.9 2.7 copy.21
  561.6 1.4 copy.20
  (35 shorter events, 6.8 us)
Async XLA Ops:
  7.2 10.7 %copy-start = (bf16[512,1792]{1,0:T(8,128)(2,1)S(1)}, bf16[512,1792]{1,0:T(8,128)(2,1)}, u32[]{:S(2)}) copy-start(bf16[512,1792]{1,0:T(8,128)(2,1)} %param.7) | copy-start | bytes 5505028
  7.2 65.4 %all-gather.8.cloned.1.call-start = ((), (), s32[]{:S(2)}) async-start(), calls=%async_computation.3 | async-start | bytes 5160960 | tf_op jit(solution)/shard_map/all_gather | solution.py:82
  7.9 124.1 %all-gather.6.cloned.1.call-start = ((), (), s32[]{:S(2)}) async-start(), calls=%async_computation.2 | async-start | bytes 5160960 | tf_op jit(solution)/shard_map/all_gather | solution.py:83
  8.7 182.8 %all-gather.4.cloned.1.call-start = ((), (), s32[]{:S(2)}) async-start(), calls=%async_computation.1 | async-start | bytes 5160960 | tf_op jit(solution)/shard_map/all_gather | solution.py:84
  9.4 363.0 %reduce-scatter.4.cloned.1.call-start = ((), (), s32[]{:S(2)}) async-start(), calls=%async_computation.4 | async-start | bytes 15482880
  191.5 11.6 %slice-start = ((s8[4587520]{0:T(1024)(128)(4,1)}), s8[4194304]{0:T(1024)(128)(4,1)S(1)}, s32[]{:S(2)}) async-start(s8[4587520]{0:T(1024)(128)(4,1)} %bitcast.12), calls=%async_computation.5 | async-start | bytes 8388608
  194.9 8.2 %slice-start.1 = ((s8[4587520]{0:T(1024)(128)(4,1)}), s8[393216]{0:T(1024)(128)(4,1)S(1)}, s32[]{:S(2)}) async-start(s8[4587520]{0:T(1024)(128)(4,1)} %bitcast.12), calls=%async_computation.6 | async-start | bytes 786432
  552.2 10.8 %copy-start.1 = (bf16[512,1792]{1,0:T(8,128)(2,1)S(1)}, bf16[512,1792]{1,0:T(8,128)(2,1)}, u32[]{:S(2)}) copy-start(bf16[512,1792]{1,0:T(8,128)(2,1)} %param.7) | copy-start | bytes 5505028
Sparse Core Ops, SparseCore 0:
  9.8 62.7 all-gather.7
  74.4 57.6 all-gather.5
  133.8 57.6 all-gather.3
  227.5 144.8 reduce-scatter.3
where the time goes:
time: 573 us; the launch traced here: 570 us
  waiting for transfers between devices  291 us (51%)
  blocking collectives  176 us (31%)
  local copies, waits for them, and re-layouts  40.9 us (7%)
  matrix products  34.1 us (6%)
  between operations  13.9 us (2%)
  other arithmetic  13.4 us (2%)
    psum x1, blocking collectives, body(): totals = lax.psum(group_shard, 'rep')  176 us
    unnamed x5, waiting for transfers between devices  132 us
    all_gather x1, waiting for transfers between devices, body(): lax.all_gather(w_up, 'dom', axis=0, tiled=True)  56.2 us
    all_gather x1, waiting for transfers between devices, body(): lax.all_gather(w_down, 'dom', axis=0, tiled=True)  52.7 us
    all_gather x1, waiting for transfers between devices, body(): lax.all_gather(w_gate, 'dom', axis=0, tiled=True)  50.3 us
    unnamed x13, local copies, waits for them, and re-layouts  29 us
    dot_general x2, matrix products, times_transpose_exact(): lax.dot_general(left, right.astype(jnp.float32), (((1,), (1,)), ((), ()))...  12.6 us
  transfers between devices with their start and end apart: 4, of which 4 were waited for; matrix products, arithmetic and copies ran while one was open for 7% of the time, Pallas kernels for 0%

commit v1 on v0

v1 whole, which is shorter than its diff:
```python
import jax
import jax.numpy as jnp
from jax import lax
from jax.experimental import pallas as pl
from jax.experimental.pallas import tpu as pltpu
from jax.sharding import PartitionSpec as P

D, FF, CAP, TOK = 1792, 1280, 96, 512
ROWS = 224
MESH = pl.DeviceIdType.MESH
BF, F32 = jnp.bfloat16, jnp.float32
VMEM_LIMIT = 52 * 1024 * 1024

POS = {0: 0, 1: 1, 3: 2, 2: 3}


def coords():
    r, d = lax.axis_index("rep"), lax.axis_index("dom")
    return r // 8, (r // 2) % 4, r % 2, d // 4, d % 4


def dev(x, zh, c, zl, y):
    return (x * 8 + zh * 2 + c, zl * 4 + y)


def dot(a, b, dims=((1,), (0,))):
    return lax.dot_general(a, b, (dims, ((), ())), preferred_element_type=F32)


def iota(shape, axis):
    return lax.broadcasted_iota(jnp.int32, shape, axis)


def pick_kernel(tok, routes, codes, cot, wg, wu, wd, x_out, w_out, sel_out):
    x, _, c, _, _ = coords()
    f = 2 * x + c
    member = routes[...] == 0
    routed = jnp.max(jnp.where(member, 1.0, 0.0), axis=1, keepdims=True)
    code = jnp.sum(jnp.where(member, codes[...], 0), axis=1, keepdims=True).astype(F32)
    below = jnp.where(iota((TOK, TOK), 1) < iota((TOK, TOK), 0), 1.0, 0.0).astype(BF)
    rank = dot(below, jnp.broadcast_to(routed, (TOK, 128)).astype(BF))
    hit = (rank == iota((TOK, 128), 1).astype(F32)) & (routed > 0.0)
    sel = jnp.where(hit, 1.0, 0.0).astype(BF)
    sel_out[...] = sel
    first = ((0,), (0,))
    weight = dot(sel, jnp.broadcast_to(code, (TOK, 128)).astype(BF), first)[:CAP, :1] * (1.0 / 256.0)

    x_out[0] = dot(sel, tok[...], first)[:CAP].astype(BF)
    x_out[1] = (weight * dot(sel, cot[...], first)[:CAP]).astype(BF)

    tile = pl.multiple_of(f * 128, 128)
    last = pl.multiple_of(1024 + (f // 4) * 128, 128)
    rest = jnp.zeros((ROWS, 128), F32)
    src, dst = iota((128, 128), 0), iota((128, 128), 1)
    for part, w in enumerate((wg, wu, wd)):
        w_out[part] = w[:, pl.ds(tile, 128)]
        move = (src - (f % 4) * 32 == dst - part * 32) & (dst // 32 == part)
        rest += dot(w[:, pl.ds(last, 128)], jnp.where(move, 1.0, 0.0).astype(BF))
    w_out[3] = rest.astype(BF)


def greet(partners):
    barrier = pltpu.get_barrier_semaphore()
    for partner in partners:
        pl.semaphore_signal(barrier, inc=1, device_id=partner, device_id_type=MESH)
    pl.semaphore_wait(barrier, len(partners))


def remote(src, dst, send, recv, index, device):
    return pltpu.make_async_remote_copy(
        src_ref=src, dst_ref=dst, send_sem=send.at[index], recv_sem=recv.at[index],
        device_id=device, device_id_type=MESH,
    )


def swiglu_back(g, u, dh):
    sig = 1.0 / (1.0 + jnp.exp(-g))
    act = g * sig
    return dh * u * sig * (1.0 + g * (1.0 - sig)), dh * act, act * u


def expert_rows(lo, hi, xa, wa, grad, dp, first):
    n = (hi - lo) * CAP
    part = lambda i: wa[i].reshape(D, 128)
    picked = xa[0, lo:hi].reshape(n, D)
    scaled = xa[1, lo:hi].reshape(n, D)
    pre = dot(picked, jnp.concatenate([part(0), part(1)], axis=1))
    down = dot(scaled, jnp.concatenate([part(2), part(3)], axis=1))
    rest = dot(picked, part(3))
    lane = iota((n, 128), 1)
    rest = jnp.where(lane < 64, rest, down[:, 128:])
    dg, du, hid = swiglu_back(pre[:, :128], pre[:, 128:], down[:, :128])
    dg_r, du_r, hid_r = swiglu_back(rest, pltpu.roll(rest, 96, 1), pltpu.roll(rest, 64, 1))
    mix = jnp.where(lane < 32, dg_r, pltpu.roll(du_r, 32, 1))
    rest_p = jnp.where(lane < 64, mix, 0.0).astype(BF)
    rest_s = jnp.where((lane >= 64) & (lane < 96), pltpu.roll(hid_r, 64, 1), 0.0).astype(BF)
    up = jnp.concatenate([dg, du], axis=1).astype(BF)
    low = jnp.concatenate([hid.astype(BF), rest_s], axis=1)
    back = jnp.concatenate([up, rest_p], axis=1)

    def columns(k, carry):
        at = pl.multiple_of(k * 256, 256)
        p_k = xa[0, lo:hi, :, pl.ds(at, 256)].reshape(n, 256)
        s_k = xa[1, lo:hi, :, pl.ds(at, 256)].reshape(n, 256)
        gu = dot(p_k, up, ((0,), (0,)))
        hr = dot(s_k, low, ((0,), (0,)))
        rr = dot(p_k, rest_p, ((0,), (0,)))
        terms = (gu[:, :128], gu[:, 128:], hr[:, :128], hr[:, 128:] + rr)
        for i, term in enumerate(terms):
            if first:
                grad[i, pl.ds(at, 256), :] = term
            else:
                grad[i, pl.ds(at, 256), :] += term
        return carry

    lax.fori_loop(0, D // 256, columns, 0)
    for k in range(D // 256):
        flat = jnp.concatenate([wa.at[i].reshape(D, 128)[k * 256:(k + 1) * 256] for i in (0, 1, 3)], axis=1)
        out = dot(back, flat, ((1,), (1,))).astype(BF)
        dp[lo:hi, :, k * 256:(k + 1) * 256] = out.reshape(hi - lo, CAP, 256)


def expert_kernel(x_ref, w_ref, gb, dp, xa, wa, grad, local, ts, tr, ws, wr):
    x, zh, c, zl, y = coords()
    sib = dev(x, zh, 1 - c, zl, y)
    right, left = dev((x + 1) % 4, zh, c, zl, y), dev((x + 3) % 4, zh, c, zl, y)
    north, south = dev(x, zh, c, zl, (y + 1) % 4), dev(x, zh, c, zl, (y + 3) % 4)
    pair = dev(x, zh, c, 1 - zl, y)
    greet([sib, right, left, north, south, pair])

    dom, dom_z = zl * 4 + y, (1 - zl) * 4 + y
    slot = lambda delta, other: 2 * POS[delta] + other

    def tsend(index, src, dst, device):
        return remote(src, dst, ts, tr, index, device)

    def wsend(index, src, dst, device):
        return remote(src, dst, ws, wr, index, device)

    own = (
        pltpu.make_async_copy(x_ref, xa.at[:, 0], local.at[0]),
        pltpu.make_async_copy(w_ref, wa.at[:, dom], local.at[1]),
    )
    p_right = tsend(0, x_ref.at[0], xa.at[0, slot(3, 0)], right)
    s_left = tsend(1, x_ref.at[1], xa.at[1, slot(1, 0)], left)
    s_right = tsend(2, x_ref.at[1], xa.at[1, slot(3, 0)], right)
    p_left = tsend(3, x_ref.at[0], xa.at[0, slot(1, 0)], left)
    x_sib = tsend(4, x_ref, xa.at[:, slot(0, 1)], sib)
    w_pair = wsend(0, w_ref, wa.at[:, dom], pair)
    w_north = wsend(1, w_ref, wa.at[:, dom], north)
    w_south = wsend(2, w_ref, wa.at[:, dom], south)
    for copy in (p_right, s_left, w_pair, w_north, w_south, s_right, p_left, x_sib, *own):
        copy.start()

    w_pair.wait_recv()
    z_north = wsend(3, wa.at[:, dom_z], wa.at[:, dom_z], north)
    z_south = wsend(4, wa.at[:, dom_z], wa.at[:, dom_z], south)
    z_north.start()
    z_south.start()

    def relay(index, base, up):
        if up:
            block = wa.at[0:2, base + (y + 3) % 4]
            copy = wsend(index, block, block, north)
        else:
            block = wa.at[2:4, base + (y + 1) % 4]
            copy = wsend(index, block, block, south)
        copy.start()
        return copy

    w_north.wait_recv()
    o_north = relay(5, zl * 4, True)
    w_south.wait_recv()
    o_south = relay(6, zl * 4, False)

    p_right.wait_recv()
    p_on = tsend(5, xa.at[0, slot(3, 0)], xa.at[0, slot(2, 0)], right)
    p_on.start()
    s_left.wait_recv()
    s_on = tsend(6, xa.at[1, slot(1, 0)], xa.at[1, slot(2, 0)], left)
    s_on.start()

    def share(index, kind, delta):
        copy = tsend(index, xa.at[kind, slot(delta, 0)], xa.at[kind, slot(delta, 1)], sib)
        copy.start()
        return copy

    shared = [share(7, 0, 3), share(8, 1, 1)]
    z_north.wait_recv()
    r_north = relay(7, (1 - zl) * 4, True)
    z_south.wait_recv()
    r_south = relay(8, (1 - zl) * 4, False)
    s_right.wait_recv()
    shared.append(share(9, 1, 3))
    p_left.wait_recv()
    shared.append(share(10, 0, 1))

    for copy in own:
        copy.wait()
    for copy in (o_north, o_south, r_north, r_south):
        copy.wait_recv()
    x_sib.wait_recv()
    for copy in shared:
        copy.wait_recv()
    expert_rows(0, 6, xa, wa, grad, dp, True)

    p_on.wait_recv()
    last = [share(11, 0, 2)]
    s_on.wait_recv()
    last.append(share(12, 1, 2))
    for copy in last:
        copy.wait_recv()
    expert_rows(6, 8, xa, wa, grad, dp, False)
    for d in range(8):
        gb[:, d // 4, d % 4] = grad[:, d * ROWS:(d + 1) * ROWS, :].astype(BF)

    for copy in (p_right, s_left, s_right, p_left, x_sib, p_on, s_on, *shared, *last,
                 w_pair, w_north, w_south, z_north, z_south, o_north, o_south, r_north, r_south):
        copy.wait_send()


def reduce_kernel(gb, dp, fin, dpick, dr, ds, df, ra, rb, ta, tb, low, high, zs, zr, gs, gr, es, er, ns, nr):
    x, zh, c, zl, y = coords()
    z = zh * 2 + zl
    sib = dev(x, zh, 1 - c, zl, y)
    ring = [dev((x + k) % 4, zh, c, zl, y) for k in (1, 2, 3)]
    yn, ys = (y + 1) % 4, (y + 3) % 4
    north, south = dev(x, zh, c, zl, yn), dev(x, zh, c, zl, ys)
    column = [dev(x, ((z + k) % 8) // 2, c, ((z + k) % 8) % 2, y) for k in range(1, 8)]
    greet([sib, north, south] + ring + column)
    up = lambda ref: ref.astype(F32)
    sends = []

    def send(index, src, dst, device, sems):
        copy = remote(src, dst, *sems, index, device)
        copy.start()
        sends.append(copy)
        return copy

    G, E, N = (gs, gr), (es, er), (ns, nr)
    opposite = (y + 2) % 4
    opp_n = send(0, gb.at[0:2, :, opposite], ra, north, G)
    opp_s = send(1, gb.at[2:4, :, opposite], rb, south, G)
    dir_n = send(2, gb.at[2:4, :, yn], low.at[2:4], north, G)
    dir_s = send(3, gb.at[0:2, :, ys], high.at[0:2], south, G)
    d_sib = send(0, dp.at[:, 1], dr, sib, E)

    opp_n.wait_recv()
    ta[...] = (up(ra[...]) + up(gb[0:2, :, yn])).astype(BF)
    add_n = send(4, ta, low.at[0:2], north, G)
    opp_s.wait_recv()
    tb[...] = (up(rb[...]) + up(gb[2:4, :, ys])).astype(BF)
    add_s = send(5, tb, high.at[2:4], south, G)

    d_sib.wait_recv()
    d_ring = []
    for k in (2, 1, 3):
        ds[k - 1] = (up(dr[POS[k]]) + up(dp[POS[k], 0])).astype(BF)
        d_ring.append(send(k, ds.at[k - 1], df.at[k - 1], ring[k - 1], E))

    for copy in (dir_n, dir_s, add_n, add_s):
        copy.wait_recv()
    zs[...] = (up(gb[:, :, y]) + up(low[...]) + up(high[...])).astype(BF)

    z_sum = []
    for k in (4, 3, 5, 2, 6, 1, 7):
        to = (z + k) % 8
        z_sum.append(send(5 + k, zs.at[to // 2, to % 2], zr.at[k - 1], column[k - 1], G))
    for copy in d_ring:
        copy.wait_recv()
    dpick[...] = (up(dr[0]) + up(dp[0, 0]) + up(df[0]) + up(df[1]) + up(df[2])).astype(BF)
    for copy in z_sum:
        copy.wait_recv()
    total = up(zs[zh, zl])
    for k in range(7):
        total += up(zr[k])
    fin[x, c, zh] = total.astype(BF)

    mine = fin.at[x, c, zh]
    over_z = [send(k - 1, mine, mine, dev(x, (zh + k) % 4, c, zl, y), N) for k in (1, 2, 3)]
    over_x = [[send(3 + k - 1, mine, mine, ring[k - 1], N) for k in (1, 2, 3)]]
    for k in (1, 3, 2):
        over_z[k - 1].wait_recv()
        piece = fin.at[x, c, (zh + 4 - k) % 4]
        over_x.append([send(3 + 3 * k + j - 1, piece, piece, ring[j - 1], N) for j in (1, 2, 3)])
    cores = [send(15, fin.at[x, c], fin.at[x, c], sib, N)]
    for j in (1, 3, 2):
        for copies in over_x:
            copies[j - 1].wait_recv()
        block = fin.at[(x + 4 - j) % 4, c]
        cores.append(send(15 + j, block, block, sib, N))
    for copy in cores:
        copy.wait_recv()
    for copy in sends:
        copy.wait_send()


def finish_kernel(fin, dpick, sel, d_tokens, gg, gu, gd):
    rows = jnp.concatenate([dpick[...], jnp.zeros((128 - CAP, D), BF)], axis=0)
    d_tokens[...] = dot(sel[...], rows).astype(BF)
    lane = iota((ROWS, 128), 1)
    rest = [fin[f, 3].astype(F32) for f in range(8)]
    for part, out in enumerate((gg, gu, gd)):
        for f in range(8):
            out[:, f * 128:(f + 1) * 128] = fin[f, part].astype(F32)
        for half in range(2):
            total = jnp.zeros((ROWS, 128), F32)
            for k in range(4):
                shift = ((k - part) * 32) % 128
                tile = rest[4 * half + k]
                tile = pltpu.roll(tile, shift, 1) if shift else tile
                total = jnp.where(lane // 32 == k, tile, total)
            out[:, 1024 + half * 128:1152 + half * 128] = total


def call(kernel, name, ins, outs, scratch=(), collective=None, flops=0):
    extra = {} if collective is None else dict(collective_id=collective, has_side_effects=True)
    return pl.pallas_call(
        kernel,
        name=name,
        out_shape=[jax.ShapeDtypeStruct(shape, dtype) for shape, dtype in outs],
        in_specs=[pl.BlockSpec(memory_space=pltpu.VMEM)] * ins,
        out_specs=[pl.BlockSpec(memory_space=pltpu.VMEM)] * len(outs),
        scratch_shapes=list(scratch),
        cost_estimate=pl.CostEstimate(flops=flops, bytes_accessed=8_000_000, transcendentals=0),
        compiler_params=pltpu.CompilerParams(vmem_limit_bytes=VMEM_LIMIT, **extra),
    )


def body(tokens, routes, gate_codes, cotangent, w_gate, w_up, w_down):
    dma = lambda n: pltpu.SemaphoreType.DMA((n,))
    buf = lambda *shape: pltpu.VMEM(shape, BF)
    x_own, w_own, sel = call(
        pick_kernel, "pick", 7,
        [((2, CAP, D), BF), ((4, ROWS, 128), BF), ((TOK, 128), BF)], flops=400_000_000,
    )(tokens, routes, gate_codes, cotangent, w_gate, w_up, w_down)
    gb, dp = call(
        expert_kernel, "expert", 2,
        [((4, 2, 4, ROWS, 128), BF), ((8, CAP, D), BF)],
        [buf(2, 8, CAP, D), buf(4, 8, ROWS, 128), pltpu.VMEM((4, D, 128), F32),
         dma(2), dma(13), dma(13), dma(9), dma(9)],
        collective=0, flops=3_500_000_000,
    )(x_own, w_own)
    fin, dpick = call(
        reduce_kernel, "reduce", 2,
        [((4, 2, 4, ROWS, 128), BF), ((CAP, D), BF)],
        [buf(4, CAP, D), buf(3, CAP, D), buf(3, CAP, D),
         buf(2, 2, ROWS, 128), buf(2, 2, ROWS, 128), buf(2, 2, ROWS, 128), buf(2, 2, ROWS, 128),
         buf(4, 2, ROWS, 128), buf(4, 2, ROWS, 128), buf(4, 2, ROWS, 128), buf(7, ROWS, 128),
         dma(13), dma(13), dma(4), dma(4), dma(19), dma(19)],
        collective=1,
    )(gb, dp.reshape(4, 2, CAP, D))
    return tuple(call(
        finish_kernel, "finish", 3,
        [((TOK, D), BF), ((ROWS, FF), F32), ((ROWS, FF), F32), ((ROWS, FF), F32)], flops=200_000_000,
    )(fin.reshape(8, 4, ROWS, 128), dpick, sel))


def solution(mesh):
    both, dom = P(("rep", "dom"), None), P("dom", None)
    return jax.shard_map(
        body,
        mesh=mesh,
        in_specs=(both, both, both, both, dom, dom, dom),
        out_specs=(both, dom, dom, dom),
        check_vma=False,
    )
```

time: 573 us -> 110 us (0.19)
  waiting for transfers between devices: 291 us -> 0 us
  blocking collectives: 176 us -> 0 us
  Pallas kernels: 0 us -> 104 us
  local copies, waits for them, and re-layouts: 40.9 us -> 4.9 us
  matrix products: 34.1 us -> 0 us
  other arithmetic: 13.4 us -> 0 us
  between operations: 13.9 us -> 0.67 us
    psum x1 -> x0, blocking collectives: 176 us -> none  [body(): totals = lax.psum(group_shard, 'rep')]
    all_gather x3 -> x0, waiting for transfers between devices: 159 us -> none  [the longest x1 56.2 us: body(): lax.all_gather(w_up, 'dom', axis=0, tiled=True)]
    unnamed x5 -> x0, waiting for transfers between devices: 132 us -> none
    pallas_call x0 -> x4, Pallas kernels: none -> 104 us  [the longest x1 55.7 us: body(): call(reduce_kernel, 'reduce', 2, [((4, 2, 4, ROWS, 128), BF), ((CAP, D),...]
    dot_general x8 -> x0, matrix products: 34.1 us -> none  [the longest x2 12.6 us: times_transpose_exact(): lax.dot_general(left, right.astype(jnp.float32), (((1,), (1,)), ((), ()))...]
    unnamed x13 -> x8, local copies, waits for them, and re-layouts: 29 us -> 4.9 us
    concatenate x1 -> x0, other arithmetic: 5.93 us -> none  [body(): jnp.concatenate([transpose_times_exact(picked_cols, d_gate), transpose_ti...]
  transfers between devices with their start and end apart: 4 -> 0, of which waited for: 4 -> 0; matrix products, arithmetic and copies ran while one was open for 7% -> 0% of each run, Pallas kernels for 0% -> 0%
where the time goes in v1:
time: 110 us
  Pallas kernels  104 us (95%)
  local copies, waits for them, and re-layouts  4.9 us (4%)
    pallas_call x1, Pallas kernels, body(): call(reduce_kernel, 'reduce', 2, [((4, 2, 4, ROWS, 128), BF), ((CAP, D),...  55.7 us
    pallas_call x1, Pallas kernels, body(): call(expert_kernel, 'expert', 2, [((4, 2, 4, ROWS, 128), BF), ((8, CAP, D...  39.5 us
    unnamed x8, local copies, waits for them, and re-layouts  4.9 us
    pallas_call x1, Pallas kernels, body(): call(finish_kernel, 'finish', 3, [((TOK, D), BF), ((ROWS, FF), F32), ((RO...  4.5 us
    pallas_call x1, Pallas kernels, body(): call(pick_kernel, 'pick', 7, [((2, CAP, D), BF), ((4, ROWS, 128), BF), ((...  4.37 us

profile of v1, /device:TPU:1, one launch (start us, length us, event | category | flops | bytes accessed | tf_op | source)
XLA Modules:
  0.0 109.7 jit_solution(3284854627754641015)
XLA Ops:
  0.6 0.8 copy.11.routes
  1.5 0.8 copy.12.codes
  2.3 0.0 copy-start
  2.3 1.1 copy-done
  3.4 0.0 copy-start.1
  3.4 1.1 copy-done.1
  4.5 4.4 %pick.1 = (bf16[2,96,1792]{2,1,0:T(8,128)(2,1)}, bf16[4,224,128]{2,1,0:T(8,128)(2,1)S(1)}, bf16[512,128]{1,0:T(8,128)(2,1)S(1)}) custom-call(bf16[512,1792]{1,0:T(8,128)(2,1)} %tok.1, s32[512,8]{1,0:T(8,128)S(1)} %copy.11.routes, s32[512,8]{1,0:T(8,128)S(1)} %copy.12.codes, bf16[512,1792]{1,0:T(8,128)(2,1)} %cot.1, bf16[224,1280]{1,0:T(8,128)(2,1)S(1)} %copy-done, ...), custom_call_target="tpu_custom_call" | custom-call | flops 400000000 | bytes 8000000 | tf_op jit(solution)/shard_map/pick/pallas_call | solution.py:333
  8.8 0.0 copy-start.2
  8.8 1.1 %copy-done.2 = bf16[2,96,1792]{2,1,0:T(8,128)(2,1)S(1)} copy-done((bf16[2,96,1792]{2,1,0:T(8,128)(2,1)S(1)}, bf16[2,96,1792]{2,1,0:T(8,128)(2,1)}, u32[]{:S(2)}) %copy-start.2) | copy-done | bytes 688152
  9.9 39.5 %expert.1 = (bf16[4,2,4,224,128]{4,3,2,1,0:T(8,128)(2,1)}, bf16[8,96,1792]{2,1,0:T(8,128)(2,1)}) custom-call(bf16[2,96,1792]{2,1,0:T(8,128)(2,1)S(1)} %copy-done.2, bf16[4,224,128]{2,1,0:T(8,128)(2,1)S(1)} %get-tuple-element.12.w_ref), custom_call_target="tpu_custom_call" | custom-call | flops 3500000000 | bytes 8000000 | tf_op jit(solution)/shard_map/expert/pallas_call | solution.py:337
  49.4 55.7 %reduce.1 = (bf16[4,2,4,224,128]{4,3,2,1,0:T(8,128)(2,1)}, bf16[96,1792]{1,0:T(8,128)(2,1)S(1)}) custom-call(bf16[4,2,4,224,128]{4,3,2,1,0:T(8,128)(2,1)} %get-tuple-element.13.gb, bf16[4,2,96,1792]{3,2,1,0:T(8,128)(2,1)} %bitcast.2), custom_call_target="tpu_custom_call" | custom-call | bytes 8000000 | tf_op jit(solution)/shard_map/reduce/pallas_call | solution.py:344
  105.2 4.5 %finish.1 = (bf16[512,1792]{1,0:T(8,128)(2,1)}, f32[224,1280]{1,0:T(8,128)}, f32[224,1280]{1,0:T(8,128)}, f32[224,1280]{1,0:T(8,128)}) custom-call(bf16[8,4,224,128]{3,2,1,0:T(8,128)(2,1)} %bitcast.3, bf16[96,1792]{1,0:T(8,128)(2,1)S(1)} %get-tuple-element.16.dpick, bf16[512,128]{1,0:T(8,128)(2,1)S(1)} %get-tuple-element.17.sel), custom_call_target="tpu_custom_call" | custom-call | flops 200000000 | bytes 8000000 | tf_op jit(solution)/shard_map/finish/pallas_call | solution.py:353
Async XLA Ops:
  2.3 1.1 copy-start
  3.4 1.1 copy-start.1
  8.8 1.1 %copy-start.2 = (bf16[2,96,1792]{2,1,0:T(8,128)(2,1)S(1)}, bf16[2,96,1792]{2,1,0:T(8,128)(2,1)}, u32[]{:S(2)}) copy-start(bf16[2,96,1792]{2,1,0:T(8,128)(2,1)} %get-tuple-element.11.x_ref) | copy-start | bytes 2064388

commit v2 on v0

v2 whole, which is shorter than its diff:
```python
import jax
import jax.numpy as jnp
from jax import lax
from jax.experimental import pallas as pl
from jax.experimental.pallas import tpu as pltpu
from jax.sharding import PartitionSpec as P

D, FF, CAP, TOK = 1792, 1280, 96, 512
ROWS = 224
HALF = CAP // 2
MESH = pl.DeviceIdType.MESH
BF, F32 = jnp.bfloat16, jnp.float32
VMEM_LIMIT = 56 * 1024 * 1024
CHUNKS = ((0, 80), (80, 64), (144, 48), (192, 32))
NC = len(CHUNKS)

POS = {0: 0, 1: 1, 3: 2, 2: 3}


def coords():
    r, d = lax.axis_index("rep"), lax.axis_index("dom")
    return r // 8, (r // 2) % 4, r % 2, d // 4, d % 4


def dev(x, zh, c, zl, y):
    return (x * 8 + zh * 2 + c, zl * 4 + y)


def dot(a, b, dims=((1,), (0,))):
    return lax.dot_general(a, b, (dims, ((), ())), preferred_element_type=F32)


def iota(shape, axis):
    return lax.broadcasted_iota(jnp.int32, shape, axis)


def swiglu_back(g, u, dh):
    sig = 1.0 / (1.0 + jnp.exp(-g))
    act = g * sig
    return dh * u * sig * (1.0 + g * (1.0 - sig)), dh * act, act * u


def rows_of(xa, kind, lo, hi):
    return xa[kind, lo:hi].reshape((hi - lo) * CAP, D)


def forward_picked(lo, hi, xa, wa):
    part = lambda i: wa[i].reshape(D, 128)
    picked = rows_of(xa, 0, lo, hi)
    return dot(picked, jnp.concatenate([part(0), part(1)], axis=1)), dot(picked, part(3))


def forward_scaled(lo, hi, xa, wa, pre, rest, back):
    n = (hi - lo) * CAP
    part = lambda i: wa[i].reshape(D, 128)
    down = dot(rows_of(xa, 1, lo, hi), jnp.concatenate([part(2), part(3)], axis=1))
    lane = iota((n, 128), 1)
    rest = jnp.where(lane < 64, rest, down[:, 128:])
    dg, du, hid = swiglu_back(pre[:, :128], pre[:, 128:], down[:, :128])
    dg_r, du_r, hid_r = swiglu_back(rest, pltpu.roll(rest, 96, 1), pltpu.roll(rest, 64, 1))
    mix = jnp.where(lane < 32, dg_r, pltpu.roll(du_r, 32, 1))
    rest_p = jnp.where(lane < 64, mix, 0.0).astype(BF)
    rest_s = jnp.where((lane >= 64) & (lane < 96), pltpu.roll(hid_r, 64, 1), 0.0).astype(BF)
    up = jnp.concatenate([dg, du], axis=1).astype(BF)
    low = jnp.concatenate([hid.astype(BF), rest_s], axis=1)
    back[lo * CAP:hi * CAP, :256] = up
    back[lo * CAP:hi * CAP, 256:] = rest_p
    return up, low, rest_p


def terms_of(lo, hi, xa, at, up, low, rest_p):
    n = (hi - lo) * CAP
    first = ((0,), (0,))
    p_k = xa[0, lo:hi, :, pl.ds(at, 256)].reshape(n, 256)
    s_k = xa[1, lo:hi, :, pl.ds(at, 256)].reshape(n, 256)
    gu, hr, rr = dot(p_k, up, first), dot(s_k, low, first), dot(p_k, rest_p, first)
    return gu[:, :128], gu[:, 128:], hr[:, :128], hr[:, 128:] + rr


def expert_kernel(
    routes, codes, tok_hbm, cot_hbm, wg, wu, wd, fin, dpick, sel_out,
    tok, cot, tail, xa, wa, grad, gb, back, dp, dr, ds, df, ra, rb, ta, tb, low, high, zs, zr,
    local, ts, tr, ws, wr, gs, gr, es, er, ns, nr,
):
    x, zh, c, zl, y = coords()
    z, f = zh * 2 + zl, 2 * x + c
    sib = dev(x, zh, 1 - c, zl, y)
    ring = [dev((x + k) % 4, zh, c, zl, y) for k in (1, 2, 3)]
    right, left = ring[0], ring[2]
    yn, ys = (y + 1) % 4, (y + 3) % 4
    north, south = dev(x, zh, c, zl, yn), dev(x, zh, c, zl, ys)
    column = [dev(x, ((z + k) % 8) // 2, c, ((z + k) % 8) % 2, y) for k in range(1, 8)]
    pair = dev(x, zh, c, 1 - zl, y)
    partners = [sib, north, south] + ring + column

    barrier = pltpu.get_barrier_semaphore()
    for partner in partners:
        pl.semaphore_signal(barrier, inc=1, device_id=partner, device_id_type=MESH)

    dom, dom_z = zl * 4 + y, (1 - zl) * 4 + y
    tile = pl.multiple_of(f * 128, 128)
    last = pl.multiple_of(1024 + (f // 4) * 128, 128)
    loads = [
        pltpu.make_async_copy(tok_hbm, tok, local.at[0]),
        pltpu.make_async_copy(cot_hbm, cot, local.at[1]),
    ]
    for i, w in enumerate((wg, wu, wd)):
        loads.append(pltpu.make_async_copy(w.at[:, pl.ds(tile, 128)], wa.at[i, dom], local.at[2 + i]))
        loads.append(pltpu.make_async_copy(w.at[:, pl.ds(last, 128)], tail.at[i], local.at[5 + i]))
    for copy in loads:
        copy.start()

    sends = []

    def send(sems, index, src, dst, device):
        copy = pltpu.make_async_remote_copy(
            src_ref=src, dst_ref=dst, send_sem=sems[0].at[index], recv_sem=sems[1].at[index],
            device_id=device, device_id_type=MESH,
        )
        copy.start()
        sends.append(copy)
        return copy

    T, W, G, E, N = (ts, tr), (ws, wr), (gs, gr), (es, er), (ns, nr)
    slot = lambda delta, other: 2 * POS[delta] + other

    member = routes[...] == 0
    routed = jnp.max(jnp.where(member, 1.0, 0.0), axis=0, keepdims=True)
    code = jnp.sum(jnp.where(member, codes[...], 0), axis=0, keepdims=True).astype(F32)
    before = jnp.where(iota((TOK, TOK), 0) < iota((TOK, TOK), 1), 1.0, 0.0).astype(BF)
    rank = dot(jnp.broadcast_to(routed, (16, TOK)).astype(BF), before)[:1]
    hit = (jnp.broadcast_to(rank, (CAP, TOK)) == iota((CAP, TOK), 0).astype(F32)) & (
        jnp.broadcast_to(routed, (CAP, TOK)) > 0.0)
    sel = jnp.where(hit, 1.0, 0.0)
    weight = jnp.sum(sel * code, axis=1, keepdims=True) * (1.0 / 256.0)
    sel = sel.astype(BF)
    sel_out[...] = sel
    loads[0].wait()
    xa[0, 0] = dot(sel, tok[...]).astype(BF)
    pl.semaphore_wait(barrier, len(partners))
    p_right = send(T, 0, xa.at[0, 0], xa.at[0, slot(3, 0)], right)
    p_left = send(T, 1, xa.at[0, 0], xa.at[0, slot(1, 0)], left)
    loads[1].wait()
    xa[1, 0] = (weight * dot(sel, cot[...])).astype(BF)
    s_right = send(T, 2, xa.at[1, 0], xa.at[1, slot(3, 0)], right)
    s_left = send(T, 3, xa.at[1, 0], xa.at[1, slot(1, 0)], left)

    for copy in loads[2:]:
        copy.wait()
    rest = jnp.zeros((ROWS, 128), F32)
    src, dst = iota((128, 128), 0), iota((128, 128), 1)
    for part in range(3):
        move = (src - (f % 4) * 32 == dst - part * 32) & (dst // 32 == part)
        rest += dot(tail[part], jnp.where(move, 1.0, 0.0).astype(BF))
    wa[3, dom] = rest.astype(BF)
    mine = wa.at[:, dom]
    w_pair = send(W, 0, mine, mine, pair)
    w_north = send(W, 1, mine, mine, north)
    w_south = send(W, 2, mine, mine, south)
    x_sib = send(T, 4, xa.at[:, 0], xa.at[:, slot(0, 1)], sib)

    def onward(index, kind, delta):
        lo, device = (0, right) if delta == 3 else (HALF, left)
        return send(T, index, xa.at[kind, slot(delta, 0), lo:lo + HALF],
                    xa.at[kind, slot(2, 0), lo:lo + HALF], device)

    def share(index, kind, delta):
        return send(T, index, xa.at[kind, slot(delta, 0)], xa.at[kind, slot(delta, 1)], sib)

    def relay(index, base, up):
        block = wa.at[0:2, base + ys] if up else wa.at[2:4, base + yn]
        return send(W, index, block, block, north if up else south)

    w_pair.wait_recv()
    other = wa.at[:, dom_z]
    z_north, z_south = send(W, 3, other, other, north), send(W, 4, other, other, south)
    p_right.wait_recv()
    p_on_r, share_p3 = onward(5, 0, 3), share(9, 0, 3)
    p_left.wait_recv()
    p_on_l, share_p1 = onward(6, 0, 1), share(10, 0, 1)
    w_north.wait_recv()
    o_north = relay(5, zl * 4, True)
    w_south.wait_recv()
    o_south = relay(6, zl * 4, False)
    s_right.wait_recv()
    s_on_r, share_s3 = onward(7, 1, 3), share(11, 1, 3)
    s_left.wait_recv()
    s_on_l, share_s1 = onward(8, 1, 1), share(12, 1, 1)
    z_north.wait_recv()
    r_north = relay(7, (1 - zl) * 4, True)
    z_south.wait_recv()
    r_south = relay(8, (1 - zl) * 4, False)
    for copy in (o_north, o_south, r_north, r_south, x_sib, share_p3, share_p1, share_s3, share_s1):
        copy.wait_recv()

    up6 = forward_scaled(0, 6, xa, wa, *forward_picked(0, 6, xa, wa), back)
    p_on_r.wait_recv()
    p_on_l.wait_recv()
    share_p2 = share(13, 0, 2)

    def columns(k, carry):
        at = pl.multiple_of(k * 256, 256)
        for i, term in enumerate(terms_of(0, 6, xa, at, *up6)):
            grad[i, pl.ds(at, 256), :] = term
        return carry

    lax.fori_loop(0, D // 256, columns, 0)
    s_on_r.wait_recv()
    s_on_l.wait_recv()
    share_s2 = share(14, 1, 2)
    share_p2.wait_recv()
    pre = forward_picked(6, 8, xa, wa)
    share_s2.wait_recv()
    up2 = forward_scaled(6, 8, xa, wa, *pre, back)
    for k in range(D // 256):
        lo = k * 256
        for i, term in enumerate(terms_of(6, 8, xa, lo, *up2)):
            total = (grad[i, lo:lo + 256, :] + term).astype(BF)
            at = lo
            while at < lo + 256:
                d, r = at // ROWS, at % ROWS
                n = min(ROWS - r, lo + 256 - at)
                gb[i, d // 4, d % 4, r:r + n, :] = total[at - lo:at - lo + n]
                at += n

    f32 = lambda ref: ref.astype(F32)
    opposite = (y + 2) % 4
    opp, direct, added, z_sum, over_z, over_x, cores = ({} for _ in range(7))

    def rows(s):
        return pl.ds(*CHUNKS[s])

    def send_opposite(s):
        if s < NC:
            r = rows(s)
            opp[s] = (send(G, 13 * s, gb.at[0:2, :, opposite, r], ra.at[:, :, r], north),
                      send(G, 13 * s + 1, gb.at[2:4, :, opposite, r], rb.at[:, :, r], south))

    def send_direct(s):
        if s < NC:
            r = rows(s)
            direct[s] = (send(G, 13 * s + 2, gb.at[2:4, :, yn, r], low.at[2:4, :, r], north),
                         send(G, 13 * s + 3, gb.at[0:2, :, ys, r], high.at[0:2, :, r], south))

    def add_y(s):
        r = rows(s)
        opp[s][0].wait_recv()
        ta[:, :, r] = (f32(ra[:, :, r]) + f32(gb[0:2, :, yn, r])).astype(BF)
        add_n = send(G, 13 * s + 4, ta.at[:, :, r], low.at[0:2, :, r], north)
        opp[s][1].wait_recv()
        tb[:, :, r] = (f32(rb[:, :, r]) + f32(gb[2:4, :, ys, r])).astype(BF)
        added[s] = (add_n, send(G, 13 * s + 5, tb.at[:, :, r], high.at[2:4, :, r], south))
        send_direct(s + 1)
        send_opposite(s + 2)

    def sum_y(s):
        r = rows(s)
        for copy in direct[s] + added[s]:
            copy.wait_recv()
        zs[:, :, r] = (f32(gb[:, :, y, r]) + f32(low[:, :, r]) + f32(high[:, :, r])).astype(BF)
        z_sum[s] = []
        for k in (4, 3, 5, 2, 6, 1, 7):
            to = (z + k) % 8
            z_sum[s].append(send(G, 13 * s + 5 + k, zs.at[to // 2, to % 2, r], zr.at[k - 1, r],
                                 column[k - 1]))

    def to_ring(s, k, q):
        piece = fin.at[x, c, q, rows(s)]
        return [send(N, 19 * s + 3 + 3 * k + j - 1, piece, piece, ring[j - 1]) for j in (1, 2, 3)]

    def sum_z(s):
        r = rows(s)
        for copy in z_sum[s]:
            copy.wait_recv()
        total = f32(zs[zh, zl, r])
        for k in range(7):
            total += f32(zr[k, r])
        fin[x, c, zh, r] = total.astype(BF)
        piece = fin.at[x, c, zh, r]
        over_z[s] = [send(N, 19 * s + k - 1, piece, piece, dev(x, (zh + k) % 4, c, zl, y))
                     for k in (1, 2, 3)]
        over_x[s] = [to_ring(s, 0, zh)]

    def gather_z(s):
        for k in (1, 3, 2):
            over_z[s][k - 1].wait_recv()
            over_x[s].append(to_ring(s, k, (zh + 4 - k) % 4))
        block = fin.at[x, c, :, rows(s)]
        cores[s] = [send(N, 19 * s + 15, block, block, sib)]

    def gather_x(s):
        for j in (1, 3, 2):
            for copies in over_x[s]:
                copies[j - 1].wait_recv()
            block = fin.at[(x + 4 - j) % 4, c, :, rows(s)]
            cores[s].append(send(N, 19 * s + 15 + j, block, block, sib))

    send_opposite(0)
    send_direct(0)
    send_opposite(1)

    for k in range(D // 256):
        flat = jnp.concatenate([wa.at[i].reshape(D, 128)[k * 256:(k + 1) * 256] for i in (0, 1, 3)], axis=1)
        out = dot(back[...], flat, ((1,), (1,))).astype(BF)
        dp[:, :, :, k * 256:(k + 1) * 256] = out.reshape(4, 2, CAP, 256)
    d_sib = send(E, 0, dp.at[:, 1], dr, sib)

    stages = (add_y, sum_y, sum_z, gather_z, gather_x)
    d_ring = []
    for step in range(NC + len(stages) - 1):
        for lag, stage in enumerate(stages):
            if 0 <= step - lag < NC:
                stage(step - lag)
        if step == 0:
            d_sib.wait_recv()
            for k in (2, 1, 3):
                ds[k - 1] = (f32(dr[POS[k]]) + f32(dp[POS[k], 0])).astype(BF)
                d_ring.append(send(E, k, ds.at[k - 1], df.at[k - 1], ring[k - 1]))

    for copy in d_ring:
        copy.wait_recv()
    dpick[...] = (f32(dr[0]) + f32(dp[0, 0]) + f32(df[0]) + f32(df[1]) + f32(df[2])).astype(BF)
    for s in range(NC):
        for copy in cores[s]:
            copy.wait_recv()
    for copy in sends:
        copy.wait_send()


def finish_kernel(fin, dpick, sel, d_tokens, gg, gu, gd, rows, out_g, out_u, out_d, sems):
    copies = []

    def put(src, dst):
        copy = pltpu.make_async_copy(src, dst, sems.at[len(copies)])
        copy.start()
        copies.append(copy)

    lane = iota((ROWS, 128), 1)
    rest = [fin[f, 3].astype(F32) for f in range(8)]
    for part, (out, dst) in enumerate(((out_g, gg), (out_u, gu), (out_d, gd))):
        for f in range(8):
            out[:, f * 128:(f + 1) * 128] = fin[f, part].astype(F32)
        for half in range(2):
            total = jnp.zeros((ROWS, 128), F32)
            for k in range(4):
                shift = ((k - part) * 32) % 128
                tile = rest[4 * half + k]
                tile = pltpu.roll(tile, shift, 1) if shift else tile
                total = jnp.where(lane // 32 == k, tile, total)
            out[:, 1024 + half * 128:1152 + half * 128] = total
        put(out, dst)
    for k in range(4):
        at = pl.ds(k * 128, 128)
        rows[at] = dot(sel[:, at], dpick[...], ((0,), (0,))).astype(BF)
        put(rows.at[at], d_tokens.at[at])
    for copy in copies:
        copy.wait()


def call(kernel, name, ins, outs, scratch=(), collective=None, flops=0):
    extra = {} if collective is None else dict(collective_id=collective, has_side_effects=True)
    vmem, any_ = pl.BlockSpec(memory_space=pltpu.VMEM), pl.BlockSpec(memory_space=pl.ANY)
    return pl.pallas_call(
        kernel,
        name=name,
        out_shape=[jax.ShapeDtypeStruct(shape, dtype) for shape, dtype, _ in outs],
        in_specs=[vmem if inside else any_ for inside in ins],
        out_specs=[vmem if inside else any_ for _, _, inside in outs],
        scratch_shapes=list(scratch),
        cost_estimate=pl.CostEstimate(flops=flops, bytes_accessed=8_000_000, transcendentals=0),
        compiler_params=pltpu.CompilerParams(vmem_limit_bytes=VMEM_LIMIT, **extra),
    )


def body(tokens, routes, gate_codes, cotangent, w_gate, w_up, w_down):
    dma = lambda n: pltpu.SemaphoreType.DMA((n,))
    buf = lambda *shape: pltpu.VMEM(shape, BF)
    quarter = buf(2, 2, ROWS, 128)
    half = buf(4, 2, ROWS, 128)
    fin, dpick, sel = call(
        expert_kernel, "expert", (1, 1, 0, 0, 0, 0, 0),
        [((4, 2, 4, ROWS, 128), BF, 1), ((CAP, D), BF, 1), ((CAP, TOK), BF, 1)],
        [buf(TOK, D), buf(TOK, D), buf(3, ROWS, 128),
         buf(2, 8, CAP, D), buf(4, 8, ROWS, 128), pltpu.VMEM((4, D, 128), F32), buf(4, 2, 4, ROWS, 128),
         buf(8 * CAP, 384), buf(4, 2, CAP, D), buf(4, CAP, D), buf(3, CAP, D), buf(3, CAP, D),
         quarter, quarter, quarter, quarter, half, half, half, buf(7, ROWS, 128),
         dma(8), dma(15), dma(15), dma(9), dma(9), dma(13 * NC), dma(13 * NC), dma(4), dma(4),
         dma(19 * NC), dma(19 * NC)],
        collective=0, flops=4_000_000_000,
    )(routes.T, gate_codes.T, tokens, cotangent, w_gate, w_up, w_down)
    wide = pltpu.VMEM((ROWS, FF), F32)
    return tuple(call(
        finish_kernel, "finish", (1, 1, 1),
        [((TOK, D), BF, 0), ((ROWS, FF), F32, 0), ((ROWS, FF), F32, 0), ((ROWS, FF), F32, 0)],
        [buf(TOK, D), wide, wide, wide, dma(7)], flops=200_000_000,
    )(fin.reshape(8, 4, ROWS, 128), dpick, sel))


def solution(mesh):
    both, dom = P(("rep", "dom"), None), P("dom", None)
    return jax.shard_map(
        body,
        mesh=mesh,
        in_specs=(both, both, both, both, dom, dom, dom),
        out_specs=(both, dom, dom, dom),
        check_vma=False,
    )
```

time: 573 us -> 87.2 us (0.15)
  waiting for transfers between devices: 291 us -> 0 us
  blocking collectives: 176 us -> 0 us
  Pallas kernels: 0 us -> 86.3 us
  local copies, waits for them, and re-layouts: 40.9 us -> 0 us
  matrix products: 34.1 us -> 0 us
  other arithmetic: 13.4 us -> 0 us
  between operations: 13.9 us -> 0.64 us
    psum x1 -> x0, blocking collectives: 176 us -> none  [body(): totals = lax.psum(group_shard, 'rep')]
    all_gather x3 -> x0, waiting for transfers between devices: 159 us -> none  [the longest x1 56.2 us: body(): lax.all_gather(w_up, 'dom', axis=0, tiled=True)]
    unnamed x5 -> x0, waiting for transfers between devices: 132 us -> none
    pallas_call x0 -> x2, Pallas kernels: none -> 86.3 us  [the longest x1 81.8 us: body(): call(expert_kernel, 'expert', (1, 1, 0, 0, 0, 0, 0), [((4, 2, 4, ROWS, 12...]
    dot_general x8 -> x0, matrix products: 34.1 us -> none  [the longest x2 12.6 us: times_transpose_exact(): lax.dot_general(left, right.astype(jnp.float32), (((1,), (1,)), ((), ()))...]
    unnamed x13 -> x0, local copies, waits for them, and re-layouts: 29 us -> none
    concatenate x1 -> x0, other arithmetic: 5.93 us -> none  [body(): jnp.concatenate([transpose_times_exact(picked_cols, d_gate), transpose_ti...]
  transfers between devices with their start and end apart: 4 -> 0, of which waited for: 4 -> 0; matrix products, arithmetic and copies ran while one was open for 7% -> 0% of each run, Pallas kernels for 0% -> 0%
where the time goes in v2:
time: 87.2 us; the launch traced here: 86.9 us
  Pallas kernels  86.3 us (99%)
    pallas_call x1, Pallas kernels, body(): call(expert_kernel, 'expert', (1, 1, 0, 0, 0, 0, 0), [((4, 2, 4, ROWS, 12...  81.8 us
    pallas_call x1, Pallas kernels, body(): call(finish_kernel, 'finish', (1, 1, 1), [((TOK, D), BF, 0), ((ROWS, FF),...  4.52 us

profile of v2, /device:TPU:1, one launch (start us, length us, event | category | flops | bytes accessed | tf_op | source)
XLA Modules:
  0.0 86.9 jit_solution(8863283644731608063)
XLA Ops:
  0.6 81.8 %expert.1 = (bf16[4,2,4,224,128]{4,3,2,1,0:T(8,128)(2,1)}, bf16[96,1792]{1,0:T(8,128)(2,1)}, bf16[96,512]{1,0:T(8,128)(2,1)}) custom-call(s32[8,512]{1,0:T(8,128)} %bitcast.4, s32[8,512]{1,0:T(8,128)} %bitcast.5, bf16[512,1792]{1,0:T(8,128)(2,1)} %tok_hbm.1, bf16[512,1792]{1,0:T(8,128)(2,1)} %cot_hbm.1, bf16[224,1280]{1,0:T(8,128)(2,1)} %wg.1, ...), custom_call_target="tpu_custom_call" | custom-call | flops 4000000000 | bytes 8000000 | tf_op jit(solution)/shard_map/expert/pallas_call | solution.py:380
  82.4 4.5 %finish.1 = (bf16[512,1792]{1,0:T(8,128)(2,1)}, f32[224,1280]{1,0:T(8,128)}, f32[224,1280]{1,0:T(8,128)}, f32[224,1280]{1,0:T(8,128)}) custom-call(bf16[8,4,224,128]{3,2,1,0:T(8,128)(2,1)} %bitcast.3, bf16[96,1792]{1,0:T(8,128)(2,1)} %get-tuple-element.8.dpick, bf16[96,512]{1,0:T(8,128)(2,1)} %get-tuple-element.9.sel), custom_call_target="tpu_custom_call" | custom-call | flops 200000000 | bytes 8000000 | tf_op jit(solution)/shard_map/finish/pallas_call | solution.py:392

commit v3 on v2

--- a/solution.py
+++ b/solution.py
@@ -11,8 +11,20 @@
 MESH = pl.DeviceIdType.MESH
 BF, F32 = jnp.bfloat16, jnp.float32
 VMEM_LIMIT = 56 * 1024 * 1024
-CHUNKS = ((0, 80), (80, 64), (144, 48), (192, 32))
+CHUNKS = (
+    (0, 48, "z", "steps"),
+    (48, 96, "relay", "steps"),
+    (144, 48, "relay", "steps"),
+    (192, 32, "direct", "once"),
+)
 NC = len(CHUNKS)
+PLAN = (
+    ("z_first", 0), ("opp", 1), ("near", 1), ("opp", 2), ("d_cores", 0),
+    ("add", 1), ("near", 2), ("straight", 3), ("d_chips", 0), ("add", 2),
+    ("z_sum", 0), ("sum_y", 1), ("sum_y", 2), ("y_sum", 0), ("sum_y", 3),
+    ("sum_z", 1), ("onto_x", 0), ("sum_z", 2), ("onto_x", 1), ("sum_z", 3), ("onto_x", 2),
+    ("onto_core", 0), ("onto_core", 1), ("onto_x", 3), ("onto_core", 2), ("onto_core", 3),
+)
 
 POS = {0: 0, 1: 1, 3: 2, 2: 3}
 
@@ -79,7 +91,7 @@
 
 def expert_kernel(
     routes, codes, tok_hbm, cot_hbm, wg, wu, wd, fin, dpick, sel_out,
-    tok, cot, tail, xa, wa, grad, gb, back, dp, dr, ds, df, ra, rb, ta, tb, low, high, zs, zr,
+    tok, cot, tail, xa, wa, grad, gb, back, dp, dr, ds, df, ra, rb, ta, tb, low, mid, high, zs, zr, zw, zy, yr,
     local, ts, tr, ws, wr, gs, gr, es, er, ns, nr,
 ):
     x, zh, c, zl, y = coords()
@@ -225,103 +237,143 @@
 
     f32 = lambda ref: ref.astype(F32)
     opposite = (y + 2) % 4
-    opp, direct, added, z_sum, over_z, over_x, cores = ({} for _ in range(7))
+    ways = [dev(x, zh, c, zl, (y + k) % 4) for k in (1, 2, 3)]
+    got = {}
 
     def rows(s):
-        return pl.ds(*CHUNKS[s])
-
-    def send_opposite(s):
-        if s < NC:
-            r = rows(s)
-            opp[s] = (send(G, 13 * s, gb.at[0:2, :, opposite, r], ra.at[:, :, r], north),
-                      send(G, 13 * s + 1, gb.at[2:4, :, opposite, r], rb.at[:, :, r], south))
-
-    def send_direct(s):
-        if s < NC:
-            r = rows(s)
-            direct[s] = (send(G, 13 * s + 2, gb.at[2:4, :, yn, r], low.at[2:4, :, r], north),
-                         send(G, 13 * s + 3, gb.at[0:2, :, ys, r], high.at[0:2, :, r], south))
-
-    def add_y(s):
-        r = rows(s)
-        opp[s][0].wait_recv()
+        return pl.ds(CHUNKS[s][0], CHUNKS[s][1])
+
+    def opp(s):
+        r = rows(s)
+        got[s, "opp"] = (send(G, 13 * s, gb.at[0:2, :, opposite, r], ra.at[:, :, r], north),
+                         send(G, 13 * s + 1, gb.at[2:4, :, opposite, r], rb.at[:, :, r], south))
+
+    def near(s):
+        r = rows(s)
+        got[s, "y"] = [send(G, 13 * s + 2, gb.at[2:4, :, yn, r], low.at[2:4, :, r], north),
+                       send(G, 13 * s + 3, gb.at[0:2, :, ys, r], high.at[0:2, :, r], south)]
+
+    def add(s):
+        r = rows(s)
+        got[s, "opp"][0].wait_recv()
         ta[:, :, r] = (f32(ra[:, :, r]) + f32(gb[0:2, :, yn, r])).astype(BF)
-        add_n = send(G, 13 * s + 4, ta.at[:, :, r], low.at[0:2, :, r], north)
-        opp[s][1].wait_recv()
+        got[s, "y"].append(send(G, 13 * s + 4, ta.at[:, :, r], low.at[0:2, :, r], north))
+        got[s, "opp"][1].wait_recv()
         tb[:, :, r] = (f32(rb[:, :, r]) + f32(gb[2:4, :, ys, r])).astype(BF)
-        added[s] = (add_n, send(G, 13 * s + 5, tb.at[:, :, r], high.at[2:4, :, r], south))
-        send_direct(s + 1)
-        send_opposite(s + 2)
+        got[s, "y"].append(send(G, 13 * s + 5, tb.at[:, :, r], high.at[2:4, :, r], south))
+
+    def straight(s):
+        r = rows(s)
+        got[s, "y"] = [send(G, 13 * s + k, gb.at[:, :, (y + k) % 4, r], to.at[:, :, r], ways[k - 1])
+                       for k, to in ((2, mid), (1, low), (3, high))]
 
     def sum_y(s):
         r = rows(s)
-        for copy in direct[s] + added[s]:
+        for copy in got[s, "y"]:
             copy.wait_recv()
-        zs[:, :, r] = (f32(gb[:, :, y, r]) + f32(low[:, :, r]) + f32(high[:, :, r])).astype(BF)
-        z_sum[s] = []
+        total = f32(gb[:, :, y, r]) + f32(low[:, :, r]) + f32(high[:, :, r])
+        if CHUNKS[s][2] == "direct":
+            total += f32(mid[:, :, r])
+        zs[:, :, r] = total.astype(BF)
+        got[s, "z"] = []
         for k in (4, 3, 5, 2, 6, 1, 7):
             to = (z + k) % 8
-            z_sum[s].append(send(G, 13 * s + 5 + k, zs.at[to // 2, to % 2, r], zr.at[k - 1, r],
-                                 column[k - 1]))
-
-    def to_ring(s, k, q):
-        piece = fin.at[x, c, q, rows(s)]
-        return [send(N, 19 * s + 3 + 3 * k + j - 1, piece, piece, ring[j - 1]) for j in (1, 2, 3)]
+            got[s, "z"].append(send(G, 13 * s + 5 + k, zs.at[to // 2, to % 2, r], zr.at[k - 1, r],
+                                    column[k - 1]))
 
     def sum_z(s):
         r = rows(s)
-        for copy in z_sum[s]:
+        for copy in got[s, "z"]:
             copy.wait_recv()
         total = f32(zs[zh, zl, r])
         for k in range(7):
             total += f32(zr[k, r])
         fin[x, c, zh, r] = total.astype(BF)
-        piece = fin.at[x, c, zh, r]
-        over_z[s] = [send(N, 19 * s + k - 1, piece, piece, dev(x, (zh + k) % 4, c, zl, y))
-                     for k in (1, 2, 3)]
-        over_x[s] = [to_ring(s, 0, zh)]
-
-    def gather_z(s):
-        for k in (1, 3, 2):
-            over_z[s][k - 1].wait_recv()
-            over_x[s].append(to_ring(s, k, (zh + 4 - k) % 4))
+        spread(s)
+
+    def z_first(s):
+        r = rows(s)
+        got[s, "z"] = []
+        for k in (4, 3, 5, 2, 6, 1, 7):
+            to = (z + k) % 8
+            got[s, "z"].append(send(G, 13 * s + 5 + k, gb.at[to // 2, to % 2, :, r], zw.at[k - 1, :, r],
+                                    column[k - 1]))
+
+    def z_sum(s):
+        r = rows(s)
+        for copy in got[s, "z"]:
+            copy.wait_recv()
+        total = f32(gb[zh, zl, :, r])
+        for k in range(7):
+            total += f32(zw[k, :, r])
+        zy[:, r] = total.astype(BF)
+        got[s, "y"] = [send(G, 13 * s + k, zy.at[(y + k) % 4, r], yr.at[k - 1, r], ways[k - 1])
+                       for k in (2, 1, 3)]
+
+    def y_sum(s):
+        r = rows(s)
+        for copy in got[s, "y"]:
+            copy.wait_recv()
+        fin[x, c, zh, r] = (f32(zy[y, r]) + f32(yr[0, r]) + f32(yr[1, r]) + f32(yr[2, r])).astype(BF)
+        spread(s)
+
+    def spread(s):
+        piece = fin.at[x, c, zh, rows(s)]
+        if CHUNKS[s][3] == "steps":
+            got[s, "zh"] = [send(N, 19 * s + k - 1, piece, piece, dev(x, (zh + k) % 4, c, zl, y))
+                            for k in (1, 2, 3)]
+            got[s, "x"] = {(j, 0): send(N, 19 * s + 2 + j, piece, piece, ring[j - 1]) for j in (2, 1, 3)}
+        else:
+            got[s, "x"] = {}
+            for j, k in ((2, 2), (1, 2), (3, 2), (2, 1), (2, 3), (0, 2), (1, 1), (1, 3), (3, 1), (3, 3),
+                         (2, 0), (0, 1), (0, 3), (1, 0), (3, 0)):
+                got[s, "x"][j, k] = send(N, 19 * s + 4 * k + j - 1, piece, piece,
+                                         dev((x + j) % 4, (zh + k) % 4, c, zl, y))
+
+    def onto_x(s):
+        if CHUNKS[s][3] == "steps":
+            for k in (1, 3, 2):
+                got[s, "zh"][k - 1].wait_recv()
+                piece = fin.at[x, c, (zh + 4 - k) % 4, rows(s)]
+                for j in (2, 1, 3):
+                    got[s, "x"][j, k] = send(N, 19 * s + 2 + 3 * k + j, piece, piece, ring[j - 1])
+        else:
+            for k in (1, 3, 2):
+                got[s, "x"][0, k].wait_recv()
         block = fin.at[x, c, :, rows(s)]
-        cores[s] = [send(N, 19 * s + 15, block, block, sib)]
-
-    def gather_x(s):
+        got[s, "core"] = [send(N, 19 * s + 15, block, block, sib)]
+
+    def onto_core(s):
         for j in (1, 3, 2):
-            for copies in over_x[s]:
-                copies[j - 1].wait_recv()
+            for k in range(4):
+                got[s, "x"][j, k].wait_recv()
             block = fin.at[(x + 4 - j) % 4, c, :, rows(s)]
-            cores[s].append(send(N, 19 * s + 15 + j, block, block, sib))
-
-    send_opposite(0)
-    send_direct(0)
-    send_opposite(1)
-
-    for k in range(D // 256):
-        flat = jnp.concatenate([wa.at[i].reshape(D, 128)[k * 256:(k + 1) * 256] for i in (0, 1, 3)], axis=1)
-        out = dot(back[...], flat, ((1,), (1,))).astype(BF)
-        dp[:, :, :, k * 256:(k + 1) * 256] = out.reshape(4, 2, CAP, 256)
-    d_sib = send(E, 0, dp.at[:, 1], dr, sib)
-
-    stages = (add_y, sum_y, sum_z, gather_z, gather_x)
-    d_ring = []
-    for step in range(NC + len(stages) - 1):
-        for lag, stage in enumerate(stages):
-            if 0 <= step - lag < NC:
-                stage(step - lag)
-        if step == 0:
-            d_sib.wait_recv()
-            for k in (2, 1, 3):
-                ds[k - 1] = (f32(dr[POS[k]]) + f32(dp[POS[k], 0])).astype(BF)
-                d_ring.append(send(E, k, ds.at[k - 1], df.at[k - 1], ring[k - 1]))
-
-    for copy in d_ring:
-        copy.wait_recv()
+            got[s, "core"].append(send(N, 19 * s + 15 + j, block, block, sib))
+
+    def d_cores(_):
+        for k in range(D // 256):
+            flat = jnp.concatenate(
+                [wa.at[i].reshape(D, 128)[k * 256:(k + 1) * 256] for i in (0, 1, 3)], axis=1)
+            out = dot(back[...], flat, ((1,), (1,))).astype(BF)
+            dp[:, :, :, k * 256:(k + 1) * 256] = out.reshape(4, 2, CAP, 256)
+        got["d"] = send(E, 0, dp.at[:, 1], dr, sib)
+
+    def d_chips(_):
+        got["d"].wait_recv()
+        for k in (2, 1, 3):
+            ds[k - 1] = (f32(dr[POS[k]]) + f32(dp[POS[k], 0])).astype(BF)
+            got["d", k] = send(E, k, ds.at[k - 1], df.at[k - 1], ring[k - 1])
+
+    for stage, s in PLAN:
+        dict(opp=opp, near=near, add=add, straight=straight, sum_y=sum_y, sum_z=sum_z, z_first=z_first,
+             z_sum=z_sum, y_sum=y_sum, onto_x=onto_x, onto_core=onto_core, d_cores=d_cores,
+             d_chips=d_chips)[stage](s)
+
+    for k in (1, 2, 3):
+        got["d", k].wait_recv()
     dpick[...] = (f32(dr[0]) + f32(dp[0, 0]) + f32(df[0]) + f32(df[1]) + f32(df[2])).astype(BF)
     for s in range(NC):
-        for copy in cores[s]:
+        for copy in got[s, "core"]:
             copy.wait_recv()
     for copy in sends:
         copy.wait_send()
@@ -383,7 +435,8 @@
         [buf(TOK, D), buf(TOK, D), buf(3, ROWS, 128),
          buf(2, 8, CAP, D), buf(4, 8, ROWS, 128), pltpu.VMEM((4, D, 128), F32), buf(4, 2, 4, ROWS, 128),
          buf(8 * CAP, 384), buf(4, 2, CAP, D), buf(4, CAP, D), buf(3, CAP, D), buf(3, CAP, D),
-         quarter, quarter, quarter, quarter, half, half, half, buf(7, ROWS, 128),
+         quarter, quarter, quarter, quarter, half, half, half, half, buf(7, ROWS, 128),
+         buf(7, 4, ROWS, 128), buf(4, ROWS, 128), buf(3, ROWS, 128),
          dma(8), dma(15), dma(15), dma(9), dma(9), dma(13 * NC), dma(13 * NC), dma(4), dma(4),
          dma(19 * NC), dma(19 * NC)],
         collective=0, flops=4_000_000_000,

time: 87.2 us -> 85.5 us (0.981)
  Pallas kernels: 86.3 us -> 84.6 us
    pallas_call x1, Pallas kernels: 81.8 us -> 80.1 us  [body(): call(expert_kernel, 'expert', (1, 1, 0, 0, 0, 0, 0), [((4, 2, 4, ROWS, 12...]
where the time goes in v3:
time: 85.5 us; the launch traced here: 85.2 us
  Pallas kernels  84.6 us (99%)
    pallas_call x1, Pallas kernels, body(): call(expert_kernel, 'expert', (1, 1, 0, 0, 0, 0, 0), [((4, 2, 4, ROWS, 12...  80.1 us
    pallas_call x1, Pallas kernels, body(): call(finish_kernel, 'finish', (1, 1, 1), [((TOK, D), BF, 0), ((ROWS, FF),...  4.52 us

profile of v3, /device:TPU:1, one launch (start us, length us, event | category | flops | bytes accessed | tf_op | source)
XLA Modules:
  0.0 85.2 jit_solution(10542828611708456059)
XLA Ops:
  0.6 80.1 %expert.1 = (bf16[4,2,4,224,128]{4,3,2,1,0:T(8,128)(2,1)}, bf16[96,1792]{1,0:T(8,128)(2,1)}, bf16[96,512]{1,0:T(8,128)(2,1)}) custom-call(s32[8,512]{1,0:T(8,128)} %bitcast.4, s32[8,512]{1,0:T(8,128)} %bitcast.5, bf16[512,1792]{1,0:T(8,128)(2,1)} %tok_hbm.1, bf16[512,1792]{1,0:T(8,128)(2,1)} %cot_hbm.1, bf16[224,1280]{1,0:T(8,128)(2,1)} %wg.1, ...), custom_call_target="tpu_custom_call" | custom-call | flops 4000000000 | bytes 8000000 | tf_op jit(solution)/shard_map/expert/pallas_call | solution.py:432
  80.7 4.5 %finish.1 = (bf16[512,1792]{1,0:T(8,128)(2,1)}, f32[224,1280]{1,0:T(8,128)}, f32[224,1280]{1,0:T(8,128)}, f32[224,1280]{1,0:T(8,128)}) custom-call(bf16[8,4,224,128]{3,2,1,0:T(8,128)(2,1)} %bitcast.3, bf16[96,1792]{1,0:T(8,128)(2,1)} %get-tuple-element.8.dpick, bf16[96,512]{1,0:T(8,128)(2,1)} %get-tuple-element.9.sel), custom_call_target="tpu_custom_call" | custom-call | flops 200000000 | bytes 8000000 | tf_op jit(solution)/shard_map/finish/pallas_call | solution.py:445

commit v4 on v3

--- a/solution.py
+++ b/solution.py
@@ -23,7 +23,8 @@
     ("add", 1), ("near", 2), ("straight", 3), ("d_chips", 0), ("add", 2),
     ("z_sum", 0), ("sum_y", 1), ("sum_y", 2), ("y_sum", 0), ("sum_y", 3),
     ("sum_z", 1), ("onto_x", 0), ("sum_z", 2), ("onto_x", 1), ("sum_z", 3), ("onto_x", 2),
-    ("onto_core", 0), ("onto_core", 1), ("onto_x", 3), ("onto_core", 2), ("onto_core", 3),
+    ("onto_core", 0), ("onto_core", 1), ("d_sum", 0), ("onto_x", 3), ("leave", 0), ("onto_core", 2),
+    ("leave", 1), ("onto_core", 3), ("leave", 2), ("leave", 3),
 )
 
 POS = {0: 0, 1: 1, 3: 2, 2: 3}
@@ -90,8 +91,8 @@
 
 
 def expert_kernel(
-    routes, codes, tok_hbm, cot_hbm, wg, wu, wd, fin, dpick, sel_out,
-    tok, cot, tail, xa, wa, grad, gb, back, dp, dr, ds, df, ra, rb, ta, tb, low, mid, high, zs, zr, zw, zy, yr,
+    routes, codes, tok_hbm, cot_hbm, wg, wu, wd, fin_hbm, dpick_hbm, sel_hbm,
+    fin, dpick, sel_own, tok, cot, tail, xa, wa, grad, gb, back, dp, dr, ds, df, ra, rb, ta, tb, low, mid, high, zs, zr, zw, zy, yr,
     local, ts, tr, ws, wr, gs, gr, es, er, ns, nr,
 ):
     x, zh, c, zl, y = coords()
@@ -122,7 +123,12 @@
     for copy in loads:
         copy.start()
 
-    sends = []
+    sends, outs = [], []
+
+    def out(src, dst):
+        copy = pltpu.make_async_copy(src, dst, local.at[8 + len(outs)])
+        copy.start()
+        outs.append(copy)
 
     def send(sems, index, src, dst, device):
         copy = pltpu.make_async_remote_copy(
@@ -146,17 +152,10 @@
     sel = jnp.where(hit, 1.0, 0.0)
     weight = jnp.sum(sel * code, axis=1, keepdims=True) * (1.0 / 256.0)
     sel = sel.astype(BF)
-    sel_out[...] = sel
+    sel_own[...] = sel
+    out(sel_own, sel_hbm)
     loads[0].wait()
     xa[0, 0] = dot(sel, tok[...]).astype(BF)
-    pl.semaphore_wait(barrier, len(partners))
-    p_right = send(T, 0, xa.at[0, 0], xa.at[0, slot(3, 0)], right)
-    p_left = send(T, 1, xa.at[0, 0], xa.at[0, slot(1, 0)], left)
-    loads[1].wait()
-    xa[1, 0] = (weight * dot(sel, cot[...])).astype(BF)
-    s_right = send(T, 2, xa.at[1, 0], xa.at[1, slot(3, 0)], right)
-    s_left = send(T, 3, xa.at[1, 0], xa.at[1, slot(1, 0)], left)
-
     for copy in loads[2:]:
         copy.wait()
     rest = jnp.zeros((ROWS, 128), F32)
@@ -165,11 +164,12 @@
         move = (src - (f % 4) * 32 == dst - part * 32) & (dst // 32 == part)
         rest += dot(tail[part], jnp.where(move, 1.0, 0.0).astype(BF))
     wa[3, dom] = rest.astype(BF)
-    mine = wa.at[:, dom]
-    w_pair = send(W, 0, mine, mine, pair)
-    w_north = send(W, 1, mine, mine, north)
-    w_south = send(W, 2, mine, mine, south)
-    x_sib = send(T, 4, xa.at[:, 0], xa.at[:, slot(0, 1)], sib)
+    loads[1].wait()
+    xa[1, 0] = (weight * dot(sel, cot[...])).astype(BF)
+
+    def weights(index, half, dom_y, device):
+        block = wa.at[2 * half:2 * half + 2, dom_y]
+        return send(W, index, block, block, device)
 
     def onward(index, kind, delta):
         lo, device = (0, right) if delta == 3 else (HALF, left)
@@ -179,30 +179,39 @@
     def share(index, kind, delta):
         return send(T, index, xa.at[kind, slot(delta, 0)], xa.at[kind, slot(delta, 1)], sib)
 
-    def relay(index, base, up):
-        block = wa.at[0:2, base + ys] if up else wa.at[2:4, base + yn]
-        return send(W, index, block, block, north if up else south)
-
-    w_pair.wait_recv()
-    other = wa.at[:, dom_z]
-    z_north, z_south = send(W, 3, other, other, north), send(W, 4, other, other, south)
+    here, there = zl * 4, (1 - zl) * 4
+    pl.semaphore_wait(barrier, len(partners))
+    p_right = send(T, 0, xa.at[0, 0], xa.at[0, slot(3, 0)], right)
+    p_left = send(T, 1, xa.at[0, 0], xa.at[0, slot(1, 0)], left)
+    north_0, south_1 = weights(0, 0, dom, north), weights(1, 1, dom, south)
+    pair_0, pair_1 = weights(2, 0, dom, pair), weights(3, 1, dom, pair)
+    north_1, south_0 = weights(4, 1, dom, north), weights(5, 0, dom, south)
+    s_right = send(T, 2, xa.at[1, 0], xa.at[1, slot(3, 0)], right)
+    s_left = send(T, 3, xa.at[1, 0], xa.at[1, slot(1, 0)], left)
+    x_sib = send(T, 4, xa.at[:, 0], xa.at[:, slot(0, 1)], sib)
+
+    north_0.wait_recv()
+    all_w = [weights(6, 0, here + ys, north)]
+    south_1.wait_recv()
+    all_w.append(weights(7, 1, here + yn, south))
+    pair_0.wait_recv()
+    z_north_0 = weights(8, 0, dom_z, north)
+    pair_1.wait_recv()
+    z_south_1 = weights(9, 1, dom_z, south)
+    all_w += [weights(10, 1, dom_z, north), weights(11, 0, dom_z, south), north_1, south_0]
     p_right.wait_recv()
     p_on_r, share_p3 = onward(5, 0, 3), share(9, 0, 3)
     p_left.wait_recv()
     p_on_l, share_p1 = onward(6, 0, 1), share(10, 0, 1)
-    w_north.wait_recv()
-    o_north = relay(5, zl * 4, True)
-    w_south.wait_recv()
-    o_south = relay(6, zl * 4, False)
+    z_north_0.wait_recv()
+    all_w.append(weights(12, 0, there + ys, north))
+    z_south_1.wait_recv()
+    all_w.append(weights(13, 1, there + yn, south))
     s_right.wait_recv()
     s_on_r, share_s3 = onward(7, 1, 3), share(11, 1, 3)
     s_left.wait_recv()
     s_on_l, share_s1 = onward(8, 1, 1), share(12, 1, 1)
-    z_north.wait_recv()
-    r_north = relay(7, (1 - zl) * 4, True)
-    z_south.wait_recv()
-    r_south = relay(8, (1 - zl) * 4, False)
-    for copy in (o_north, o_south, r_north, r_south, x_sib, share_p3, share_p1, share_s3, share_s1):
+    for copy in all_w + [x_sib, share_p3, share_p1, share_s3, share_s1]:
         copy.wait_recv()
 
     up6 = forward_scaled(0, 6, xa, wa, *forward_picked(0, 6, xa, wa), back)
@@ -364,22 +373,36 @@
             ds[k - 1] = (f32(dr[POS[k]]) + f32(dp[POS[k], 0])).astype(BF)
             got["d", k] = send(E, k, ds.at[k - 1], df.at[k - 1], ring[k - 1])
 
+    def d_sum(_):
+        for k in (1, 2, 3):
+            got["d", k].wait_recv()
+        total = f32(dr[0]) + f32(dp[0, 0]) + f32(df[0]) + f32(df[1]) + f32(df[2])
+        dpick[...] = total.astype(BF)
+        out(dpick, dpick_hbm)
+
+    def leave(s):
+        for copy in got[s, "core"]:
+            copy.wait_recv()
+        out(fin.at[:, :, :, rows(s)], fin_hbm.at[:, :, :, rows(s)])
+
     for stage, s in PLAN:
         dict(opp=opp, near=near, add=add, straight=straight, sum_y=sum_y, sum_z=sum_z, z_first=z_first,
              z_sum=z_sum, y_sum=y_sum, onto_x=onto_x, onto_core=onto_core, d_cores=d_cores,
-             d_chips=d_chips)[stage](s)
-
-    for k in (1, 2, 3):
-        got["d", k].wait_recv()
-    dpick[...] = (f32(dr[0]) + f32(dp[0, 0]) + f32(df[0]) + f32(df[1]) + f32(df[2])).astype(BF)
-    for s in range(NC):
-        for copy in got[s, "core"]:
-            copy.wait_recv()
+             d_chips=d_chips, d_sum=d_sum, leave=leave)[stage](s)
+
     for copy in sends:
         copy.wait_send()
-
-
-def finish_kernel(fin, dpick, sel, d_tokens, gg, gu, gd, rows, out_g, out_u, out_d, sems):
+    for copy in outs:
+        copy.wait()
+
+
+def finish_kernel(fin_hbm, dpick_hbm, sel_hbm, d_tokens, gg, gu, gd,
+                  fin, dpick, sel, rows, out_g, out_u, out_d, loaded, sems):
+    loads = [pltpu.make_async_copy(sel_hbm, sel, loaded.at[4]),
+             pltpu.make_async_copy(dpick_hbm, dpick, loaded.at[5])]
+    parts = [pltpu.make_async_copy(fin_hbm.at[:, i], fin.at[:, i], loaded.at[i]) for i in range(4)]
+    for copy in loads + [parts[i] for i in (3, 0, 1, 2)]:
+        copy.start()
     copies = []
 
     def put(src, dst):
@@ -387,9 +410,17 @@
         copy.start()
         copies.append(copy)
 
+    for copy in loads:
+        copy.wait()
+    for k in range(4):
+        at = pl.ds(k * 128, 128)
+        rows[at] = dot(sel[:, at], dpick[...], ((0,), (0,))).astype(BF)
+        put(rows.at[at], d_tokens.at[at])
     lane = iota((ROWS, 128), 1)
+    parts[3].wait()
     rest = [fin[f, 3].astype(F32) for f in range(8)]
     for part, (out, dst) in enumerate(((out_g, gg), (out_u, gu), (out_d, gd))):
+        parts[part].wait()
         for f in range(8):
             out[:, f * 128:(f + 1) * 128] = fin[f, part].astype(F32)
         for half in range(2):
@@ -401,10 +432,6 @@
                 total = jnp.where(lane // 32 == k, tile, total)
             out[:, 1024 + half * 128:1152 + half * 128] = total
         put(out, dst)
-    for k in range(4):
-        at = pl.ds(k * 128, 128)
-        rows[at] = dot(sel[:, at], dpick[...], ((0,), (0,))).astype(BF)
-        put(rows.at[at], d_tokens.at[at])
     for copy in copies:
         copy.wait()
 
@@ -431,21 +458,21 @@
     half = buf(4, 2, ROWS, 128)
     fin, dpick, sel = call(
         expert_kernel, "expert", (1, 1, 0, 0, 0, 0, 0),
-        [((4, 2, 4, ROWS, 128), BF, 1), ((CAP, D), BF, 1), ((CAP, TOK), BF, 1)],
-        [buf(TOK, D), buf(TOK, D), buf(3, ROWS, 128),
+        [((4, 2, 4, ROWS, 128), BF, 0), ((CAP, D), BF, 0), ((CAP, TOK), BF, 0)],
+        [buf(4, 2, 4, ROWS, 128), buf(CAP, D), buf(CAP, TOK), buf(TOK, D), buf(TOK, D), buf(3, ROWS, 128),
          buf(2, 8, CAP, D), buf(4, 8, ROWS, 128), pltpu.VMEM((4, D, 128), F32), buf(4, 2, 4, ROWS, 128),
          buf(8 * CAP, 384), buf(4, 2, CAP, D), buf(4, CAP, D), buf(3, CAP, D), buf(3, CAP, D),
          quarter, quarter, quarter, quarter, half, half, half, half, buf(7, ROWS, 128),
          buf(7, 4, ROWS, 128), buf(4, ROWS, 128), buf(3, ROWS, 128),
-         dma(8), dma(15), dma(15), dma(9), dma(9), dma(13 * NC), dma(13 * NC), dma(4), dma(4),
+         dma(10 + NC), dma(15), dma(15), dma(14), dma(14), dma(13 * NC), dma(13 * NC), dma(4), dma(4),
          dma(19 * NC), dma(19 * NC)],
         collective=0, flops=4_000_000_000,
     )(routes.T, gate_codes.T, tokens, cotangent, w_gate, w_up, w_down)
     wide = pltpu.VMEM((ROWS, FF), F32)
     return tuple(call(
-        finish_kernel, "finish", (1, 1, 1),
+        finish_kernel, "finish", (0, 0, 0),
         [((TOK, D), BF, 0), ((ROWS, FF), F32, 0), ((ROWS, FF), F32, 0), ((ROWS, FF), F32, 0)],
-        [buf(TOK, D), wide, wide, wide, dma(7)], flops=200_000_000,
+        [buf(8, 4, ROWS, 128), buf(CAP, D), buf(CAP, TOK), buf(TOK, D), wide, wide, wide, dma(6), dma(7)], flops=200_000_000,
     )(fin.reshape(8, 4, ROWS, 128), dpick, sel))
 
 

time: 85.5 us -> 81.5 us (0.953)
  Pallas kernels: 84.6 us -> 80.6 us
    pallas_call x1, Pallas kernels: 80.1 us -> 76.7 us  [body(): call(expert_kernel, 'expert', (1, 1, 0, 0, 0, 0, 0), [((4, 2, 4, ROWS, 12...]
where the time goes in v4:
time: 81.5 us; the launch traced here: 81.2 us
  Pallas kernels  80.6 us (99%)
    pallas_call x1, Pallas kernels, body(): call(expert_kernel, 'expert', (1, 1, 0, 0, 0, 0, 0), [((4, 2, 4, ROWS, 12...  76.7 us
    pallas_call x1, Pallas kernels, body(): call(finish_kernel, 'finish', (0, 0, 0), [((TOK, D), BF, 0), ((ROWS, FF),...  3.83 us

profile of v4, /device:TPU:1, one launch (start us, length us, event | category | flops | bytes accessed | tf_op | source)
XLA Modules:
  0.0 81.2 jit_solution(6752410279182578768)
XLA Ops:
  0.6 76.7 %expert.1 = (bf16[4,2,4,224,128]{4,3,2,1,0:T(8,128)(2,1)}, bf16[96,1792]{1,0:T(8,128)(2,1)}, bf16[96,512]{1,0:T(8,128)(2,1)}) custom-call(s32[8,512]{1,0:T(8,128)} %bitcast.4, s32[8,512]{1,0:T(8,128)} %bitcast.5, bf16[512,1792]{1,0:T(8,128)(2,1)} %tok_hbm.1, bf16[512,1792]{1,0:T(8,128)(2,1)} %cot_hbm.1, bf16[224,1280]{1,0:T(8,128)(2,1)} %wg.1, ...), custom_call_target="tpu_custom_call" | custom-call | flops 4000000000 | bytes 8000000 | tf_op jit(solution)/shard_map/expert/pallas_call | solution.py:459
  77.4 3.8 %finish.1 = (bf16[512,1792]{1,0:T(8,128)(2,1)}, f32[224,1280]{1,0:T(8,128)}, f32[224,1280]{1,0:T(8,128)}, f32[224,1280]{1,0:T(8,128)}) custom-call(bf16[8,4,224,128]{3,2,1,0:T(8,128)(2,1)} %bitcast.3, bf16[96,1792]{1,0:T(8,128)(2,1)} %get-tuple-element.8.dpick_hbm, bf16[96,512]{1,0:T(8,128)(2,1)} %get-tuple-element.9.sel_hbm), custom_call_target="tpu_custom_call" | custom-call | flops 200000000 | bytes 8000000 | tf_op jit(solution)/shard_map/finish/pallas_call | solution.py:472

commit v5 on v4

--- a/solution.py
+++ b/solution.py
@@ -13,18 +13,19 @@
 VMEM_LIMIT = 56 * 1024 * 1024
 CHUNKS = (
     (0, 48, "z", "steps"),
-    (48, 96, "relay", "steps"),
-    (144, 48, "relay", "steps"),
-    (192, 32, "direct", "once"),
+    (48, 48, "relay", "steps"),
+    (96, 64, "relay", "steps"),
+    (160, 32, "relay", "steps"),
+    (192, 32, "relay", "once"),
 )
 NC = len(CHUNKS)
 PLAN = (
-    ("z_first", 0), ("opp", 1), ("near", 1), ("opp", 2), ("d_cores", 0),
-    ("add", 1), ("near", 2), ("straight", 3), ("d_chips", 0), ("add", 2),
-    ("z_sum", 0), ("sum_y", 1), ("sum_y", 2), ("y_sum", 0), ("sum_y", 3),
-    ("sum_z", 1), ("onto_x", 0), ("sum_z", 2), ("onto_x", 1), ("sum_z", 3), ("onto_x", 2),
-    ("onto_core", 0), ("onto_core", 1), ("d_sum", 0), ("onto_x", 3), ("leave", 0), ("onto_core", 2),
-    ("leave", 1), ("onto_core", 3), ("leave", 2), ("leave", 3),
+    ("z_first", 0), ("opp", 1), ("near", 1), ("opp", 2), ("d_cores", 0), ("add", 1), ("near", 2), ("opp", 3),
+    ("d_chips", 0), ("add", 2), ("near", 3), ("opp", 4), ("sum_y", 1), ("add", 3), ("near", 4), ("sum_y", 2),
+    ("add", 4), ("z_sum", 0), ("sum_y", 3), ("sum_z", 1), ("sum_y", 4), ("y_sum", 0), ("sum_z", 2),
+    ("sum_z", 3), ("onto_x", 1), ("sum_z", 4), ("onto_x", 0), ("d_sum", 0), ("onto_x", 2), ("onto_x", 3),
+    ("onto_core", 1), ("leave", 1), ("onto_core", 0), ("onto_x", 4), ("onto_core", 4), ("leave", 0),
+    ("onto_core", 2), ("leave", 4), ("onto_core", 3), ("leave", 2), ("leave", 3),
 )
 
 POS = {0: 0, 1: 1, 3: 2, 2: 3}
@@ -93,7 +94,7 @@
 def expert_kernel(
     routes, codes, tok_hbm, cot_hbm, wg, wu, wd, fin_hbm, dpick_hbm, sel_hbm,
     fin, dpick, sel_own, tok, cot, tail, xa, wa, grad, gb, back, dp, dr, ds, df, ra, rb, ta, tb, low, mid, high, zs, zr, zw, zy, yr,
-    local, ts, tr, ws, wr, gs, gr, es, er, ns, nr,
+    local, ts, tr, ws, wr, gs, gr, es, er, ns, nr, told,
 ):
     x, zh, c, zl, y = coords()
     z, f = zh * 2 + zl, 2 * x + c
@@ -104,7 +105,8 @@
     north, south = dev(x, zh, c, zl, yn), dev(x, zh, c, zl, ys)
     column = [dev(x, ((z + k) % 8) // 2, c, ((z + k) % 8) % 2, y) for k in range(1, 8)]
     pair = dev(x, zh, c, 1 - zl, y)
-    partners = [sib, north, south] + ring + column
+    nearby = [right, left, north, south, column[0], column[6]]
+    partners = [sib] + nearby
 
     barrier = pltpu.get_barrier_semaphore()
     for partner in partners:
@@ -179,6 +181,10 @@
     def share(index, kind, delta):
         return send(T, index, xa.at[kind, slot(delta, 0)], xa.at[kind, slot(delta, 1)], sib)
 
+    def tell(index, devices):
+        for device in devices:
+            pl.semaphore_signal(told.at[index], inc=1, device_id=device, device_id_type=MESH)
+
     here, there = zl * 4, (1 - zl) * 4
     pl.semaphore_wait(barrier, len(partners))
     p_right = send(T, 0, xa.at[0, 0], xa.at[0, slot(3, 0)], right)
@@ -190,6 +196,7 @@
     s_left = send(T, 3, xa.at[1, 0], xa.at[1, slot(1, 0)], left)
     x_sib = send(T, 4, xa.at[:, 0], xa.at[:, slot(0, 1)], sib)
 
+    tell(0, nearby)
     north_0.wait_recv()
     all_w = [weights(6, 0, here + ys, north)]
     south_1.wait_recv()
@@ -199,6 +206,8 @@
     pair_1.wait_recv()
     z_south_1 = weights(9, 1, dom_z, south)
     all_w += [weights(10, 1, dom_z, north), weights(11, 0, dom_z, south), north_1, south_0]
+    pl.semaphore_wait(told.at[0], len(nearby))
+    tell(1, (column[0], column[6]))
     p_right.wait_recv()
     p_on_r, share_p3 = onward(5, 0, 3), share(9, 0, 3)
     p_left.wait_recv()
@@ -207,10 +216,13 @@
     all_w.append(weights(12, 0, there + ys, north))
     z_south_1.wait_recv()
     all_w.append(weights(13, 1, there + yn, south))
+    pl.semaphore_wait(told.at[1], 2)
+    tell(2, (column[0], column[6]))
     s_right.wait_recv()
     s_on_r, share_s3 = onward(7, 1, 3), share(11, 1, 3)
     s_left.wait_recv()
     s_on_l, share_s1 = onward(8, 1, 1), share(12, 1, 1)
+    pl.semaphore_wait(told.at[2], 2)
     for copy in all_w + [x_sib, share_p3, share_p1, share_s3, share_s1]:
         copy.wait_recv()
 
@@ -465,7 +477,8 @@
          quarter, quarter, quarter, quarter, half, half, half, half, buf(7, ROWS, 128),
          buf(7, 4, ROWS, 128), buf(4, ROWS, 128), buf(3, ROWS, 128),
          dma(10 + NC), dma(15), dma(15), dma(14), dma(14), dma(13 * NC), dma(13 * NC), dma(4), dma(4),
-         dma(19 * NC), dma(19 * NC)],
+         dma(19 * NC), dma(19 * NC),
+         pltpu.SemaphoreType.REGULAR((3,))],
         collective=0, flops=4_000_000_000,
     )(routes.T, gate_codes.T, tokens, cotangent, w_gate, w_up, w_down)
     wide = pltpu.VMEM((ROWS, FF), F32)

time: 81.5 us -> 79.5 us (0.975)
  Pallas kernels: 80.6 us -> 78.6 us
    pallas_call x1, Pallas kernels: 76.7 us -> 74.8 us  [body(): call(expert_kernel, 'expert', (1, 1, 0, 0, 0, 0, 0), [((4, 2, 4, ROWS, 12...]
where the time goes in v5:
time: 79.5 us; the launch traced here: 79.3 us
  Pallas kernels  78.6 us (99%)
    pallas_call x1, Pallas kernels, body(): call(expert_kernel, 'expert', (1, 1, 0, 0, 0, 0, 0), [((4, 2, 4, ROWS, 12...  74.8 us
    pallas_call x1, Pallas kernels, body(): call(finish_kernel, 'finish', (0, 0, 0), [((TOK, D), BF, 0), ((ROWS, FF),...  3.83 us

profile of v5, /device:TPU:1, one launch (start us, length us, event | category | flops | bytes accessed | tf_op | source)
XLA Modules:
  0.0 79.3 jit_solution(8904313454136247734)
XLA Ops:
  0.6 74.8 %expert.1 = (bf16[4,2,4,224,128]{4,3,2,1,0:T(8,128)(2,1)}, bf16[96,1792]{1,0:T(8,128)(2,1)}, bf16[96,512]{1,0:T(8,128)(2,1)}) custom-call(s32[8,512]{1,0:T(8,128)} %bitcast.4, s32[8,512]{1,0:T(8,128)} %bitcast.5, bf16[512,1792]{1,0:T(8,128)(2,1)} %tok_hbm.1, bf16[512,1792]{1,0:T(8,128)(2,1)} %cot_hbm.1, bf16[224,1280]{1,0:T(8,128)(2,1)} %wg.1, ...), custom_call_target="tpu_custom_call" | custom-call | flops 4000000000 | bytes 8000000 | tf_op jit(solution)/shard_map/expert/pallas_call | solution.py:471
  75.4 3.8 %finish.1 = (bf16[512,1792]{1,0:T(8,128)(2,1)}, f32[224,1280]{1,0:T(8,128)}, f32[224,1280]{1,0:T(8,128)}, f32[224,1280]{1,0:T(8,128)}) custom-call(bf16[8,4,224,128]{3,2,1,0:T(8,128)(2,1)} %bitcast.3, bf16[96,1792]{1,0:T(8,128)(2,1)} %get-tuple-element.8.dpick_hbm, bf16[96,512]{1,0:T(8,128)(2,1)} %get-tuple-element.9.sel_hbm), custom_call_target="tpu_custom_call" | custom-call | flops 200000000 | bytes 8000000 | tf_op jit(solution)/shard_map/finish/pallas_call | solution.py:485

commit v6 on v5

--- a/solution.py
+++ b/solution.py
@@ -158,6 +158,30 @@
     out(sel_own, sel_hbm)
     loads[0].wait()
     xa[0, 0] = dot(sel, tok[...]).astype(BF)
+    def weights(index, half, dom_y, device):
+        block = wa.at[2 * half:2 * half + 2, dom_y]
+        return send(W, index, block, block, device)
+
+    def around(index, kind, lo, to_right):
+        to, device = (slot(3, 0), right) if to_right else (slot(1, 0), left)
+        return send(T, index, xa.at[kind, 0, lo:lo + HALF], xa.at[kind, to, lo:lo + HALF], device)
+
+    def onward(index, kind, delta):
+        lo, device = (0, right) if delta == 3 else (HALF, left)
+        return send(T, index, xa.at[kind, slot(delta, 0), lo:lo + HALF],
+                    xa.at[kind, slot(2, 0), lo:lo + HALF], device)
+
+    def share(index, kind, delta):
+        return send(T, index, xa.at[kind, slot(delta, 0)], xa.at[kind, slot(delta, 1)], sib)
+
+    def tell(index, devices):
+        for device in devices:
+            pl.semaphore_signal(told.at[index], inc=1, device_id=device, device_id_type=MESH)
+
+    here, there = zl * 4, (1 - zl) * 4
+    pl.semaphore_wait(barrier, len(partners))
+    p_right, p_left = around(0, 0, 0, True), around(1, 0, HALF, False)
+    p_right_2, p_left_2 = around(15, 0, HALF, True), around(16, 0, 0, False)
     for copy in loads[2:]:
         copy.wait()
     rest = jnp.zeros((ROWS, 128), F32)
@@ -166,34 +190,13 @@
         move = (src - (f % 4) * 32 == dst - part * 32) & (dst // 32 == part)
         rest += dot(tail[part], jnp.where(move, 1.0, 0.0).astype(BF))
     wa[3, dom] = rest.astype(BF)
-    loads[1].wait()
-    xa[1, 0] = (weight * dot(sel, cot[...])).astype(BF)
-
-    def weights(index, half, dom_y, device):
-        block = wa.at[2 * half:2 * half + 2, dom_y]
-        return send(W, index, block, block, device)
-
-    def onward(index, kind, delta):
-        lo, device = (0, right) if delta == 3 else (HALF, left)
-        return send(T, index, xa.at[kind, slot(delta, 0), lo:lo + HALF],
-                    xa.at[kind, slot(2, 0), lo:lo + HALF], device)
-
-    def share(index, kind, delta):
-        return send(T, index, xa.at[kind, slot(delta, 0)], xa.at[kind, slot(delta, 1)], sib)
-
-    def tell(index, devices):
-        for device in devices:
-            pl.semaphore_signal(told.at[index], inc=1, device_id=device, device_id_type=MESH)
-
-    here, there = zl * 4, (1 - zl) * 4
-    pl.semaphore_wait(barrier, len(partners))
-    p_right = send(T, 0, xa.at[0, 0], xa.at[0, slot(3, 0)], right)
-    p_left = send(T, 1, xa.at[0, 0], xa.at[0, slot(1, 0)], left)
     north_0, south_1 = weights(0, 0, dom, north), weights(1, 1, dom, south)
     pair_0, pair_1 = weights(2, 0, dom, pair), weights(3, 1, dom, pair)
     north_1, south_0 = weights(4, 1, dom, north), weights(5, 0, dom, south)
-    s_right = send(T, 2, xa.at[1, 0], xa.at[1, slot(3, 0)], right)
-    s_left = send(T, 3, xa.at[1, 0], xa.at[1, slot(1, 0)], left)
+    loads[1].wait()
+    xa[1, 0] = (weight * dot(sel, cot[...])).astype(BF)
+    s_right, s_left = around(2, 1, 0, True), around(3, 1, HALF, False)
+    s_right_2, s_left_2 = around(17, 1, HALF, True), around(18, 1, 0, False)
     x_sib = send(T, 4, xa.at[:, 0], xa.at[:, slot(0, 1)], sib)
 
     tell(0, nearby)
@@ -209,9 +212,12 @@
     pl.semaphore_wait(told.at[0], len(nearby))
     tell(1, (column[0], column[6]))
     p_right.wait_recv()
-    p_on_r, share_p3 = onward(5, 0, 3), share(9, 0, 3)
+    p_on_r = onward(5, 0, 3)
     p_left.wait_recv()
-    p_on_l, share_p1 = onward(6, 0, 1), share(10, 0, 1)
+    p_on_l = onward(6, 0, 1)
+    p_right_2.wait_recv()
+    p_left_2.wait_recv()
+    share_p3, share_p1 = share(9, 0, 3), share(10, 0, 1)
     z_north_0.wait_recv()
     all_w.append(weights(12, 0, there + ys, north))
     z_south_1.wait_recv()
@@ -219,9 +225,12 @@
     pl.semaphore_wait(told.at[1], 2)
     tell(2, (column[0], column[6]))
     s_right.wait_recv()
-    s_on_r, share_s3 = onward(7, 1, 3), share(11, 1, 3)
+    s_on_r = onward(7, 1, 3)
     s_left.wait_recv()
-    s_on_l, share_s1 = onward(8, 1, 1), share(12, 1, 1)
+    s_on_l = onward(8, 1, 1)
+    s_right_2.wait_recv()
+    s_left_2.wait_recv()
+    share_s3, share_s1 = share(11, 1, 3), share(12, 1, 1)
     pl.semaphore_wait(told.at[2], 2)
     for copy in all_w + [x_sib, share_p3, share_p1, share_s3, share_s1]:
         copy.wait_recv()
@@ -476,7 +485,7 @@
          buf(8 * CAP, 384), buf(4, 2, CAP, D), buf(4, CAP, D), buf(3, CAP, D), buf(3, CAP, D),
          quarter, quarter, quarter, quarter, half, half, half, half, buf(7, ROWS, 128),
          buf(7, 4, ROWS, 128), buf(4, ROWS, 128), buf(3, ROWS, 128),
-         dma(10 + NC), dma(15), dma(15), dma(14), dma(14), dma(13 * NC), dma(13 * NC), dma(4), dma(4),
+         dma(10 + NC), dma(19), dma(19), dma(14), dma(14), dma(13 * NC), dma(13 * NC), dma(4), dma(4),
          dma(19 * NC), dma(19 * NC),
          pltpu.SemaphoreType.REGULAR((3,))],
         collective=0, flops=4_000_000_000,

time: 79.5 us -> 79.4 us (level)
  no operation moved by 1% of the time
where the time goes in v6:
time: 79.4 us; the launch traced here: 79.1 us
  Pallas kernels  78.5 us (99%)
    pallas_call x1, Pallas kernels, body(): call(expert_kernel, 'expert', (1, 1, 0, 0, 0, 0, 0), [((4, 2, 4, ROWS, 12...  74.6 us
    pallas_call x1, Pallas kernels, body(): call(finish_kernel, 'finish', (0, 0, 0), [((TOK, D), BF, 0), ((ROWS, FF),...  3.83 us

profile of v6, /device:TPU:1, one launch (start us, length us, event | category | flops | bytes accessed | tf_op | source)
XLA Modules:
  0.0 79.1 jit_solution(4208337632441485996)
XLA Ops:
  0.6 74.6 %expert.1 = (bf16[4,2,4,224,128]{4,3,2,1,0:T(8,128)(2,1)}, bf16[96,1792]{1,0:T(8,128)(2,1)}, bf16[96,512]{1,0:T(8,128)(2,1)}) custom-call(s32[8,512]{1,0:T(8,128)} %bitcast.4, s32[8,512]{1,0:T(8,128)} %bitcast.5, bf16[512,1792]{1,0:T(8,128)(2,1)} %tok_hbm.1, bf16[512,1792]{1,0:T(8,128)(2,1)} %cot_hbm.1, bf16[224,1280]{1,0:T(8,128)(2,1)} %wg.1, ...), custom_call_target="tpu_custom_call" | custom-call | flops 4000000000 | bytes 8000000 | tf_op jit(solution)/shard_map/expert/pallas_call | solution.py:480
  75.3 3.8 %finish.1 = (bf16[512,1792]{1,0:T(8,128)(2,1)}, f32[224,1280]{1,0:T(8,128)}, f32[224,1280]{1,0:T(8,128)}, f32[224,1280]{1,0:T(8,128)}) custom-call(bf16[8,4,224,128]{3,2,1,0:T(8,128)(2,1)} %bitcast.3, bf16[96,1792]{1,0:T(8,128)(2,1)} %get-tuple-element.8.dpick_hbm, bf16[96,512]{1,0:T(8,128)(2,1)} %get-tuple-element.9.sel_hbm), custom_call_target="tpu_custom_call" | custom-call | flops 200000000 | bytes 8000000 | tf_op jit(solution)/shard_map/finish/pallas_call | solution.py:494

commit v7 on v6

--- a/solution.py
+++ b/solution.py
@@ -252,6 +252,15 @@
     share_s2 = share(14, 1, 2)
     share_p2.wait_recv()
     pre = forward_picked(6, 8, xa, wa)
+
+    def token_part(lo, hi):
+        for k in range(D // 256):
+            flat = jnp.concatenate(
+                [wa.at[i].reshape(D, 128)[k * 256:(k + 1) * 256] for i in (0, 1, 3)], axis=1)
+            part = dot(back[2 * lo * CAP:2 * hi * CAP], flat, ((1,), (1,))).astype(BF)
+            dp[lo:hi, :, :, k * 256:(k + 1) * 256] = part.reshape(hi - lo, 2, CAP, 256)
+
+    token_part(0, 1)
     share_s2.wait_recv()
     up2 = forward_scaled(6, 8, xa, wa, *pre, back)
     for k in range(D // 256):
@@ -381,11 +390,7 @@
             got[s, "core"].append(send(N, 19 * s + 15 + j, block, block, sib))
 
     def d_cores(_):
-        for k in range(D // 256):
-            flat = jnp.concatenate(
-                [wa.at[i].reshape(D, 128)[k * 256:(k + 1) * 256] for i in (0, 1, 3)], axis=1)
-            out = dot(back[...], flat, ((1,), (1,))).astype(BF)
-            dp[:, :, :, k * 256:(k + 1) * 256] = out.reshape(4, 2, CAP, 256)
+        token_part(1, 4)
         got["d"] = send(E, 0, dp.at[:, 1], dr, sib)
 
     def d_chips(_):

time: 79.4 us -> 79.2 us (level)
  no operation moved by 1% of the time
where the time goes in v7:
time: 79.2 us; the launch traced here: 78.9 us
  Pallas kernels  78.2 us (99%)
    pallas_call x1, Pallas kernels, body(): call(expert_kernel, 'expert', (1, 1, 0, 0, 0, 0, 0), [((4, 2, 4, ROWS, 12...  74.4 us
    pallas_call x1, Pallas kernels, body(): call(finish_kernel, 'finish', (0, 0, 0), [((TOK, D), BF, 0), ((ROWS, FF),...  3.83 us

profile of v7, /device:TPU:1, one launch (start us, length us, event | category | flops | bytes accessed | tf_op | source)
XLA Modules:
  0.0 78.9 jit_solution(399736958543336327)
XLA Ops:
  0.6 74.4 %expert.1 = (bf16[4,2,4,224,128]{4,3,2,1,0:T(8,128)(2,1)}, bf16[96,1792]{1,0:T(8,128)(2,1)}, bf16[96,512]{1,0:T(8,128)(2,1)}) custom-call(s32[8,512]{1,0:T(8,128)} %bitcast.4, s32[8,512]{1,0:T(8,128)} %bitcast.5, bf16[512,1792]{1,0:T(8,128)(2,1)} %tok_hbm.1, bf16[512,1792]{1,0:T(8,128)(2,1)} %cot_hbm.1, bf16[224,1280]{1,0:T(8,128)(2,1)} %wg.1, ...), custom_call_target="tpu_custom_call" | custom-call | flops 4000000000 | bytes 8000000 | tf_op jit(solution)/shard_map/expert/pallas_call | solution.py:485
  75.1 3.8 %finish.1 = (bf16[512,1792]{1,0:T(8,128)(2,1)}, f32[224,1280]{1,0:T(8,128)}, f32[224,1280]{1,0:T(8,128)}, f32[224,1280]{1,0:T(8,128)}) custom-call(bf16[8,4,224,128]{3,2,1,0:T(8,128)(2,1)} %bitcast.3, bf16[96,1792]{1,0:T(8,128)(2,1)} %get-tuple-element.8.dpick_hbm, bf16[96,512]{1,0:T(8,128)(2,1)} %get-tuple-element.9.sel_hbm), custom_call_target="tpu_custom_call" | custom-call | flops 200000000 | bytes 8000000 | tf_op jit(solution)/shard_map/finish/pallas_call | solution.py:499

commit v8 on v7

--- a/solution.py
+++ b/solution.py
@@ -13,19 +13,17 @@
 VMEM_LIMIT = 56 * 1024 * 1024
 CHUNKS = (
     (0, 48, "z", "steps"),
-    (48, 48, "relay", "steps"),
-    (96, 64, "relay", "steps"),
-    (160, 32, "relay", "steps"),
+    (48, 80, "relay", "steps"),
+    (128, 64, "relay", "steps"),
     (192, 32, "relay", "once"),
 )
 NC = len(CHUNKS)
 PLAN = (
     ("z_first", 0), ("opp", 1), ("near", 1), ("opp", 2), ("d_cores", 0), ("add", 1), ("near", 2), ("opp", 3),
-    ("d_chips", 0), ("add", 2), ("near", 3), ("opp", 4), ("sum_y", 1), ("add", 3), ("near", 4), ("sum_y", 2),
-    ("add", 4), ("z_sum", 0), ("sum_y", 3), ("sum_z", 1), ("sum_y", 4), ("y_sum", 0), ("sum_z", 2),
-    ("sum_z", 3), ("onto_x", 1), ("sum_z", 4), ("onto_x", 0), ("d_sum", 0), ("onto_x", 2), ("onto_x", 3),
-    ("onto_core", 1), ("leave", 1), ("onto_core", 0), ("onto_x", 4), ("onto_core", 4), ("leave", 0),
-    ("onto_core", 2), ("leave", 4), ("onto_core", 3), ("leave", 2), ("leave", 3),
+    ("d_chips", 0), ("add", 2), ("near", 3), ("sum_y", 1), ("add", 3), ("sum_y", 2), ("z_sum", 0),
+    ("sum_y", 3), ("y_sum", 0), ("sum_z", 1), ("sum_z", 2), ("sum_z", 3), ("onto_x", 0), ("d_sum", 0),
+    ("onto_x", 1), ("onto_x", 2), ("onto_core", 0), ("leave", 0), ("onto_x", 3), ("onto_core", 3),
+    ("onto_core", 1), ("leave", 3), ("onto_core", 2), ("leave", 1), ("leave", 2),
 )
 
 POS = {0: 0, 1: 1, 3: 2, 2: 3}

time: 79.2 us -> 79.3 us (level)
  no operation moved by 1% of the time
where the time goes in v8:
time: 79.3 us; the launch traced here: 79 us
  Pallas kernels  78.4 us (99%)
    pallas_call x1, Pallas kernels, body(): call(expert_kernel, 'expert', (1, 1, 0, 0, 0, 0, 0), [((4, 2, 4, ROWS, 12...  74.5 us
    pallas_call x1, Pallas kernels, body(): call(finish_kernel, 'finish', (0, 0, 0), [((TOK, D), BF, 0), ((ROWS, FF),...  3.83 us

profile of v8, /device:TPU:1, one launch (start us, length us, event | category | flops | bytes accessed | tf_op | source)
XLA Modules:
  0.0 79.0 jit_solution(14086596765806260031)
XLA Ops:
  0.6 74.5 %expert.1 = (bf16[4,2,4,224,128]{4,3,2,1,0:T(8,128)(2,1)}, bf16[96,1792]{1,0:T(8,128)(2,1)}, bf16[96,512]{1,0:T(8,128)(2,1)}) custom-call(s32[8,512]{1,0:T(8,128)} %bitcast.4, s32[8,512]{1,0:T(8,128)} %bitcast.5, bf16[512,1792]{1,0:T(8,128)(2,1)} %tok_hbm.1, bf16[512,1792]{1,0:T(8,128)(2,1)} %cot_hbm.1, bf16[224,1280]{1,0:T(8,128)(2,1)} %wg.1, ...), custom_call_target="tpu_custom_call" | custom-call | flops 4000000000 | bytes 8000000 | tf_op jit(solution)/shard_map/expert/pallas_call | solution.py:483
  75.2 3.8 %finish.1 = (bf16[512,1792]{1,0:T(8,128)(2,1)}, f32[224,1280]{1,0:T(8,128)}, f32[224,1280]{1,0:T(8,128)}, f32[224,1280]{1,0:T(8,128)}) custom-call(bf16[8,4,224,128]{3,2,1,0:T(8,128)(2,1)} %bitcast.3, bf16[96,1792]{1,0:T(8,128)(2,1)} %get-tuple-element.8.dpick_hbm, bf16[96,512]{1,0:T(8,128)(2,1)} %get-tuple-element.9.sel_hbm), custom_call_target="tpu_custom_call" | custom-call | flops 200000000 | bytes 8000000 | tf_op jit(solution)/shard_map/finish/pallas_call | solution.py:497
